TPU v7x, 32 devices: a whole 2x2x4 slice. The times are simulated.
32 devices in a mesh: row: 8 (over y, x, core), col: 4 (over z).
Axes of the slice: x: 2, y: 2, z: 4, core: 2. Of those that a mesh axis runs over, the one named last changes fastest.
Arguments:
- pair: bfloat16 [512, 512, 128], P('row', 'col'), may hold values from -6 to 6
- ln_gain: float32 [128], replicated, may hold values from 0.1 to 1.9
- ln_bias: float32 [128], replicated, may hold values from -3 to 3
- gate_weight: bfloat16 [128, 512], replicated, may hold values from -0.5 to 0.5
- up_weight: bfloat16 [128, 512], replicated, may hold values from -0.5 to 0.5
- out_weight: bfloat16 [512, 128], replicated, may hold values from -0.25 to 0.25
- head_weight: bfloat16 [128, 64], replicated, may hold values from -1 to 1
- targets: int32 [512, 512], P(('row', 'col')), may hold values from 0 to 63
- pair_mask: int32 [512, 512], P(('row', 'col')), may hold values 0 or 1
Outputs:
- pair_out: bfloat16 [512, 512, 128], P('row', 'col')
- loss: float32 [], replicated
- grad_gain: float32 [128], replicated
- grad_bias: float32 [128], replicated
- grad_gate: float32 [128, 512], replicated
- grad_up: float32 [128, 512], replicated
- grad_out: float32 [512, 128], replicated
- grad_head: float32 [128, 64], replicated
All inputs are finite; a program needn't handle non-finite values. No bound on the sum of `pair_mask` on one device may be relied on, other than what follows from the above.
Results may differ from a plain program's by a relative error of at most 0.001.
The roundings to bfloat16 on the way count: a program that leaves them out, or rounds other values in their place, can miss the bound.
Values may be sent and summed in bfloat16 or wider, within the bound.
A program may use at most 64 MiB of HBM per device.

v0:
```python
import math

import jax
import jax.numpy as jnp
from jax import lax
from jax.sharding import PartitionSpec as P

EPSILON = 1e-05


def normalize(rows_in, ln_gain, ln_bias):
    values = rows_in.astype(jnp.float32)
    centered = values - jnp.mean(values, axis=-1, keepdims=True)
    variance = jnp.mean(centered * centered, axis=-1, keepdims=True)
    unit_rows = centered * lax.rsqrt(variance + EPSILON)
    normed = (unit_rows * ln_gain + ln_bias).astype(jnp.bfloat16)
    return (unit_rows, normed)


def inner(left, right):
    return lax.dot_general(
        left, right, (((0,), (0,)), ((), ())), preferred_element_type=jnp.float32
    )


def advance(rows_in, ln_gain, ln_bias, gate_weight, up_weight, out_weight):
    unit_rows, normed = normalize(rows_in, ln_gain, ln_bias)
    gate_pre = jnp.dot(normed, gate_weight, preferred_element_type=jnp.float32)
    up_pre = jnp.dot(normed, up_weight, preferred_element_type=jnp.float32)
    hidden = (jax.nn.silu(gate_pre) * up_pre).astype(jnp.bfloat16)
    update = jnp.dot(hidden, out_weight, preferred_element_type=jnp.float32)
    return (rows_in.astype(jnp.float32) + update).astype(jnp.bfloat16)


def retreat(totals, rows_in, grad_rows, ln_gain, ln_bias, gate_weight, up_weight, out_weight):
    unit_rows, normed = normalize(rows_in, ln_gain, ln_bias)
    gate_pre = jnp.dot(normed, gate_weight, preferred_element_type=jnp.float32)
    up_pre = jnp.dot(normed, up_weight, preferred_element_type=jnp.float32)
    squashed = jax.nn.sigmoid(gate_pre)
    silu_val = gate_pre * squashed
    hidden = (silu_val * up_pre).astype(jnp.bfloat16)
    grad_hidden = jnp.dot(grad_rows, out_weight.T, preferred_element_type=jnp.float32)
    grad_gate_pre = (grad_hidden * up_pre * squashed * (1.0 + gate_pre * (1.0 - squashed))).astype(
        jnp.bfloat16
    )
    grad_up_pre = (grad_hidden * silu_val).astype(jnp.bfloat16)
    grad_normed = jnp.dot(
        grad_gate_pre, gate_weight.T, preferred_element_type=jnp.float32
    ) + jnp.dot(grad_up_pre, up_weight.T, preferred_element_type=jnp.float32)
    sum_gain, sum_bias, sum_gate, sum_up, sum_out = totals
    return (
        sum_gain + jnp.sum(grad_normed * unit_rows, axis=0),
        sum_bias + jnp.sum(grad_normed, axis=0),
        sum_gate + inner(normed, grad_gate_pre),
        sum_up + inner(normed, grad_up_pre),
        sum_out + inner(hidden, grad_rows),
    )


def loss_terms(logits, targets, pair_mask):
    bins = logits.shape[-1]
    one_hot = (targets[..., None] == jnp.arange(bins, dtype=jnp.int32)).astype(jnp.float32)
    log_total = jnp.log(jnp.sum(jnp.exp(logits), axis=-1))
    weights_mask = pair_mask.astype(jnp.float32)
    loss_part = jnp.sum(weights_mask * (log_total - jnp.sum(logits * one_hot, axis=-1)))
    soft_probs = jnp.exp(logits - log_total[..., None])
    return (loss_part, soft_probs)


def grad_from(soft_probs, targets, pair_mask, tokens):
    bins = soft_probs.shape[-1]
    one_hot = (targets[..., None] == jnp.arange(bins, dtype=jnp.int32)).astype(jnp.float32)
    weights_mask = pair_mask.astype(jnp.float32)
    return (weights_mask[..., None] * (soft_probs - one_hot) / tokens).astype(jnp.bfloat16)


def shards(
    pair, ln_gain, ln_bias, gate_weight, up_weight, out_weight, head_weight, targets, pair_mask
):
    rows_tile, cols_tile, width = pair.shape
    tokens = cols_tile * lax.axis_size("col")
    block_rows = math.gcd(rows_tile, max(1, 2048 // cols_tile))
    count = rows_tile // block_rows
    blocks = pair.reshape(count, block_rows * cols_tile, width)

    def forward_one(rows_in):
        return advance(rows_in, ln_gain, ln_bias, gate_weight, up_weight, out_weight)

    pair_out = lax.map(forward_one, blocks).reshape(pair.shape)
    half_tile = jnp.dot(pair_out, head_weight, preferred_element_type=jnp.float32).astype(
        jnp.bfloat16
    )
    half_rows = lax.all_to_all(half_tile, "col", split_axis=0, concat_axis=1, tiled=True)
    half_back, target_back, mask_back = (
        lax.all_to_all(
            jnp.swapaxes(half_rows, 0, 1), ("row", "col"), split_axis=0, concat_axis=1, tiled=True
        ),
        lax.all_to_all(
            jnp.swapaxes(targets, 0, 1), ("row", "col"), split_axis=0, concat_axis=1, tiled=True
        ),
        lax.all_to_all(
            jnp.swapaxes(pair_mask, 0, 1), ("row", "col"), split_axis=0, concat_axis=1, tiled=True
        ),
    )
    half_flip, target_tile, mask_tile, target_turn, mask_turn = (
        lax.all_to_all(half_back, "col", split_axis=1, concat_axis=0, tiled=True),
        lax.all_to_all(targets, "col", split_axis=1, concat_axis=0, tiled=True),
        lax.all_to_all(pair_mask, "col", split_axis=1, concat_axis=0, tiled=True),
        lax.all_to_all(target_back, "col", split_axis=1, concat_axis=0, tiled=True),
        lax.all_to_all(mask_back, "col", split_axis=1, concat_axis=0, tiled=True),
    )
    logits = half_tile.astype(jnp.float32) + half_flip.astype(jnp.float32)
    loss_part, soft_probs = loss_terms(logits, target_tile, mask_tile)
    tile_grad = grad_from(soft_probs, target_tile, mask_tile, tokens)
    tile_flip = grad_from(soft_probs, target_turn, mask_turn, tokens)
    bins = head_weight.shape[1]
    flat_out = pair_out.reshape(-1, width)
    grad_head = inner(flat_out, tile_grad.reshape(-1, bins)) + inner(
        flat_out, tile_flip.reshape(-1, bins)
    )
    head_back = head_weight.T
    grad_pair = (
        jnp.dot(tile_grad, head_back, preferred_element_type=jnp.float32)
        + jnp.dot(tile_flip, head_back, preferred_element_type=jnp.float32)
    ).astype(jnp.bfloat16)
    grad_blocks = grad_pair.reshape(count, block_rows * cols_tile, width)
    hidden_width = gate_weight.shape[1]
    start = (
        jnp.zeros((width,), jnp.float32),
        jnp.zeros((width,), jnp.float32),
        jnp.zeros((width, hidden_width), jnp.float32),
        jnp.zeros((width, hidden_width), jnp.float32),
        jnp.zeros((hidden_width, width), jnp.float32),
    )

    def backward_one(totals, inputs):
        return (
            retreat(
                totals, inputs[0], inputs[1], ln_gain, ln_bias, gate_weight, up_weight, out_weight
            ),
            None,
        )

    totals, unused = lax.scan(backward_one, start, (blocks, grad_blocks))
    summed = lax.psum(
        (loss_part, totals[0], totals[1], totals[2], totals[3], totals[4], grad_head),
        ("row", "col"),
    )
    loss = summed[0] / (tokens * tokens)
    return (pair_out, loss, summed[1], summed[2], summed[3], summed[4], summed[5], summed[6])


def solution(mesh):
    placed = (
        P("row", "col", None),
        P(),
        P(),
        P(),
        P(),
        P(),
        P(),
        P(("row", "col"), None),
        P(("row", "col"), None),
    )
    return jax.shard_map(
        shards,
        mesh=mesh,
        in_specs=placed,
        out_specs=(P("row", "col", None), P(), P(), P(), P(), P(), P(), P()),
        check_vma=False,
    )
```

profile of v0, /device:TPU:0, one launch (start us, length us, event | category | flops | bytes accessed | tf_op | source)
XLA Modules:
  0.0 409.0 jit_solution(18171355809929681514)
XLA Ops:
  8.6 6.3 %all-to-all-start = ((s32[16,4,128]{2,0,1:T(8,128)}), s32[16,4,128]{2,0,1:T(8,128)S(1)}, u32[]{:S(2)}, u32[]{:S(2)}) async-start(s32[16,4,128]{2,0,1:T(8,128)} %copy_bitcast_fusion.2), calls=%async_computation | async-start | bytes 65536 | tf_op jit(solution)/shard_map/all_to_all | solution.py:108
  14.9 47.0 %while.29 = (s32[]{:T(128)}, bf16[4,2048,128]{2,1,0:T(8,128)(2,1)}, bf16[4,2048,128]{2,1,0:T(8,128)(2,1)}, f32[128]{0:T(128)}, f32[128]{0:T(128)}, /*index=5*/bf...) while((s32[]{:T(128)}, bf16[4,2048,128]{2,1,0:T(8,128)(2,1)}, ...), condition=%wide.region_3.4_spmd, body=%wide.region_0.3_spmd.sunk | while | flops 817104896 | bytes 21462268 | solution.py:89
  17.9 4.0 fusion.131
  21.9 4.7 %fusion.132 = bf16[4,2048,128]{2,1,0:T(8,128)(2,1)} fusion(bf16[4,2048,128]{2,1,0:T(8,128)(2,1)} %get-tuple-element.380, s32[]{:T(128)S(6)} %copy.120, bf16[512,128]{1,0:T(8,128)(2,1)S(1)} %copy-done.27, f32[2048,512]{1,0:T(8,128)} %fusion.131, bf16[128,512]{1,0:T(8,128)(2,1)S(1)} %copy-done.8, f32[128]{0:T(128)S(1)} %copy-done.13, ...), kind=kOutput, calls=%fused_computation.4.clone.1 | convolution fusion | flops 545521664 | bytes 6047744 | tf_op jit(solution)/shard_map/while/body/eval_jaxpr/dot_general | solution.py:31
  29.6 4.0 fusion.131
  33.6 4.7 %fusion.132 = bf16[4,2048,128]{2,1,0:T(8,128)(2,1)} fusion(bf16[4,2048,128]{2,1,0:T(8,128)(2,1)} %get-tuple-element.380, s32[]{:T(128)S(6)} %copy.120, bf16[512,128]{1,0:T(8,128)(2,1)S(1)} %copy-done.27, f32[2048,512]{1,0:T(8,128)} %fusion.131, bf16[128,512]{1,0:T(8,128)(2,1)S(1)} %copy-done.8, f32[128]{0:T(128)S(1)} %copy-done.13, ...), kind=kOutput, calls=%fused_computation.4.clone.1 | convolution fusion | flops 545521664 | bytes 6047744 | tf_op jit(solution)/shard_map/while/body/eval_jaxpr/dot_general | solution.py:31
  41.4 4.0 fusion.131
  45.4 4.7 %fusion.132 = bf16[4,2048,128]{2,1,0:T(8,128)(2,1)} fusion(bf16[4,2048,128]{2,1,0:T(8,128)(2,1)} %get-tuple-element.380, s32[]{:T(128)S(6)} %copy.120, bf16[512,128]{1,0:T(8,128)(2,1)S(1)} %copy-done.27, f32[2048,512]{1,0:T(8,128)} %fusion.131, bf16[128,512]{1,0:T(8,128)(2,1)S(1)} %copy-done.8, f32[128]{0:T(128)S(1)} %copy-done.13, ...), kind=kOutput, calls=%fused_computation.4.clone.1 | convolution fusion | flops 545521664 | bytes 6047744 | tf_op jit(solution)/shard_map/while/body/eval_jaxpr/dot_general | solution.py:31
  53.1 4.0 fusion.131
  57.1 4.7 %fusion.132 = bf16[4,2048,128]{2,1,0:T(8,128)(2,1)} fusion(bf16[4,2048,128]{2,1,0:T(8,128)(2,1)} %get-tuple-element.380, s32[]{:T(128)S(6)} %copy.120, bf16[512,128]{1,0:T(8,128)(2,1)S(1)} %copy-done.27, f32[2048,512]{1,0:T(8,128)} %fusion.131, bf16[128,512]{1,0:T(8,128)(2,1)S(1)} %copy-done.8, f32[128]{0:T(128)S(1)} %copy-done.13, ...), kind=kOutput, calls=%fused_computation.4.clone.1 | convolution fusion | flops 545521664 | bytes 6047744 | tf_op jit(solution)/shard_map/while/body/eval_jaxpr/dot_general | solution.py:31
  62.9 6.1 %all-to-all-start.5 = ((s32[32,1,256]{2,1,0:T(1,128)}), s32[32,1,256]{2,1,0:T(1,128)S(1)}, u32[]{:S(2)}, u32[]{:S(2)}) async-start(s32[32,1,256]{2,1,0:T(1,128)} %reshape.122), calls=%async_computation.5 | async-start | bytes 65536 | tf_op jit(solution)/shard_map/all_to_all | solution.py:101
  69.0 3.4 convolution_convert_fusion
  72.4 3.9 all-to-all-done.5
  76.3 3.5 all-to-all-start.1
  80.9 24.8 %all-to-all-done.1 = bf16[64,128,64]{1,2,0:T(8,128)(2,1)S(1)} async-done(((bf16[64,128,64]{1,2,0:T(8,128)(2,1)}), bf16[64,128,64]{1,2,0:T(8,128)(2,1)S(1)}, u32[]{:S(2)}, u32[]{:S(2)}) %all-to-all-start.1) | async-done | bytes 1048608 | tf_op jit(solution)/shard_map/all_to_all | solution.py:93
  105.7 2.6 all-to-all-start.7
  111.6 2.3 reshape.116
  115.5 4.2 %all-to-all-start.2 = ((bf16[32,2,8192]{2,1,0:T(2,128)(2,1)}), bf16[32,2,8192]{2,1,0:T(2,128)(2,1)S(1)}, u32[]{:S(2)}, u32[]{:S(2)}) async-start(bf16[32,2,8192]{2,1,0:T(2,128)(2,1)} %reshape.116), calls=%async_computation.2 | async-start | bytes 2097152 | tf_op jit(solution)/shard_map/all_to_all | solution.py:95
  121.8 23.0 %all-to-all-done.2 = bf16[32,2,8192]{2,1,0:T(2,128)(2,1)S(1)} async-done(((bf16[32,2,8192]{2,1,0:T(2,128)(2,1)}), bf16[32,2,8192]{2,1,0:T(2,128)(2,1)S(1)}, u32[]{:S(2)}, u32[]{:S(2)}) %all-to-all-start.2) | async-done | bytes 1048608 | tf_op jit(solution)/shard_map/all_to_all | solution.py:95
  144.8 4.5 %all-to-all-start.6 = ((s32[16,4,128]{2,0,1:T(8,128)}), s32[16,4,128]{2,0,1:T(8,128)S(1)}, u32[]{:S(2)}, u32[]{:S(2)}) async-start(s32[16,4,128]{2,0,1:T(8,128)} %copy.85), calls=%async_computation.6 | async-start | bytes 65536 | tf_op jit(solution)/shard_map/all_to_all | solution.py:110
  152.5 2.7 reshape.118
  155.1 5.1 %all-to-all-start.3 = ((bf16[4,2,65536]{2,1,0:T(2,128)(2,1)}), bf16[4,2,65536]{2,1,0:T(2,128)(2,1)S(1)}, u32[]{:S(2)}, u32[]{:S(2)}) async-start(bf16[4,2,65536]{2,1,0:T(2,128)(2,1)} %reshape.118), calls=%async_computation.3 | async-start | bytes 2097152 | tf_op jit(solution)/shard_map/all_to_all | solution.py:106
  160.8 25.3 %all-to-all-done.3 = bf16[4,2,65536]{2,1,0:T(2,128)(2,1)S(1)} async-done(((bf16[4,2,65536]{2,1,0:T(2,128)(2,1)}), bf16[4,2,65536]{2,1,0:T(2,128)(2,1)S(1)}, u32[]{:S(2)}, u32[]{:S(2)}) %all-to-all-start.3) | async-done | bytes 1048608 | tf_op jit(solution)/shard_map/all_to_all | solution.py:106
  186.2 3.4 all-to-all-start.4
  198.7 4.9 %all-to-all-start.8 = ((s32[16,4,128]{2,0,1:T(8,128)}), s32[16,4,128]{2,0,1:T(8,128)S(1)}, u32[]{:S(2)}, u32[]{:S(2)}) async-start(s32[16,4,128]{2,0,1:T(8,128)} %copy.88), calls=%async_computation.8 | async-start | bytes 65536 | tf_op jit(solution)/shard_map/all_to_all | solution.py:109
  203.6 2.3 exponential_reduce_fusion
  206.6 2.7 all-to-all-done.8
  209.2 2.5 multiply_convert_fusion.7
  216.6 50.4 %while.30 = (s32[]{:T(128)}, f32[128]{0:T(128)}, f32[128]{0:T(128)}, f32[128,512]{1,0:T(8,128)}, f32[128,512]{1,0:T(8,128)S(1)}, /*index=5*/f32[512,128]{1,0:T(8...) while((s32[]{:T(128)}, f32[128]{0:T(128)}, ...), condition=%wide.region_13.14_spmd.clone, body=%wide.region_8.13_spmd.clone.sunk | while | flops 2177501440 | bytes 60584492 | solution.py:144
  222.2 2.1 multiply_convert_fusion.12
  271.3 39.5 %all-reduce = (f32[]{:T(128)}, f32[128]{0:T(128)}, f32[128]{0:T(128)}, f32[128,64]{0,1:T(8,128)}) all-reduce(f32[]{:T(128)} %fusion.67, f32[128]{0:T(128)S(1)} %copy-done.26, f32[128]{0:T(128)S(1)} %copy-done.23, f32[128,64]{0,1:T(8,128)S(1)} %convolution_add_fusion.4), channel_id=1, replica_groups=mesh['row'=8,'col'=4] {'row','col'}, use_global_device_ids=true, to_apply=%region_7.8 | all-reduce | flops 8449 | bytes 67592 | tf_op jit(solution)/shard_map/psum | solution.py:145
  311.4 84.6 %all-reduce.4.cloned.1.call-done = (f32[128,512]{1,0:T(8,128)}, f32[128,512]{1,0:T(8,128)}, f32[512,128]{1,0:T(8,128)}) async-done(((f32[128,512]{1,0:T(8,128)}, f32[128,512]{1,0:T(8,128)}, f32[512,128]{1,0:T(8,128)}), (f32[128,512]{1,0:T(8,128)}, f32[128,512]{1,0:T(8,128)}, f32[512,128]{1,0:T(8,128)})) %all-reduce.4.cloned.1.call-update) | async-done | bytes 786448 | tf_op jit(solution)/shard_map/psum | solution.py:145
  (281 shorter events, 97.4 us)
Async XLA Ops:
  7.2 61.8 %copy-start = (bf16[128,64]{0,1:T(8,128)(2,1)S(1)}, bf16[128,64]{0,1:T(8,128)(2,1)}, u32[]{:S(2)}) copy-start(bf16[128,64]{0,1:T(8,128)(2,1)} %param.19) | copy-start | bytes 49156
  8.6 54.3 %all-to-all-start = ((s32[16,4,128]{2,0,1:T(8,128)}), s32[16,4,128]{2,0,1:T(8,128)S(1)}, u32[]{:S(2)}, u32[]{:S(2)}) async-start(s32[16,4,128]{2,0,1:T(8,128)} %copy_bitcast_fusion.2), calls=%async_computation | async-start | bytes 65536 | tf_op jit(solution)/shard_map/all_to_all | solution.py:108
  14.9 47.0 %copy-start.18 = (s32[16,512]{1,0:T(8,128)S(1)}, s32[16,512]{1,0:T(8,128)}, u32[]{:S(2)}) copy-start(s32[16,512]{1,0:T(8,128)} %param.21) | copy-start | bytes 98308
  17.8 4.0 copy-start.1
  17.9 4.0 copy-start.8
  17.9 4.0 copy-start.11
  29.6 4.0 copy-start.1
  29.6 4.0 copy-start.8
  29.6 4.0 copy-start.11
  29.6 4.0 copy-start.13
  41.3 4.0 copy-start.1
  41.3 4.0 copy-start.8
  41.3 4.0 copy-start.11
  53.1 4.0 copy-start.1
  53.1 4.0 copy-start.8
  53.1 4.0 copy-start.11
  53.1 4.0 copy-start.13
  53.1 4.0 copy-start.27
  62.9 126.8 %copy-start.15 = (s32[16,4,128]{2,0,1:T(8,128)}, s32[16,4,128]{2,0,1:T(8,128)S(1)}, u32[]{:S(2)}) copy-start(s32[16,4,128]{2,0,1:T(8,128)S(1)} %all-to-all-done) | copy-start | bytes 98308
  62.9 13.4 %all-to-all-start.5 = ((s32[32,1,256]{2,1,0:T(1,128)}), s32[32,1,256]{2,1,0:T(1,128)S(1)}, u32[]{:S(2)}, u32[]{:S(2)}) async-start(s32[32,1,256]{2,1,0:T(1,128)} %reshape.122), calls=%async_computation.5 | async-start | bytes 65536 | tf_op jit(solution)/shard_map/all_to_all | solution.py:101
  69.0 10.8 %copy-start.19 = (s32[16,512]{1,0:T(8,128)S(1)}, s32[16,512]{1,0:T(8,128)}, u32[]{:S(2)}) copy-start(s32[16,512]{1,0:T(8,128)} %param.20) | copy-start | bytes 98308
  76.3 29.4 %all-to-all-start.1 = ((bf16[64,128,64]{1,2,0:T(8,128)(2,1)}), bf16[64,128,64]{1,2,0:T(8,128)(2,1)S(1)}, u32[]{:S(2)}, u32[]{:S(2)}) async-start(bf16[64,128,64]{1,2,0:T(8,128)(2,1)} %convolution_convert_fusion), calls=%async_computation.1 | async-start | bytes 2097152 | tf_op jit(solution)/shard_map/all_to_all | solution.py:93
  105.7 9.9 %all-to-all-start.7 = ((s32[32,1,256]{2,1,0:T(1,128)}), s32[32,1,256]{2,1,0:T(1,128)S(1)}, u32[]{:S(2)}, u32[]{:S(2)}) async-start(s32[32,1,256]{2,1,0:T(1,128)} %reshape.120), calls=%async_computation.7 | async-start | bytes 65536 | tf_op jit(solution)/shard_map/all_to_all | solution.py:98
  115.5 29.2 %all-to-all-start.2 = ((bf16[32,2,8192]{2,1,0:T(2,128)(2,1)}), bf16[32,2,8192]{2,1,0:T(2,128)(2,1)S(1)}, u32[]{:S(2)}, u32[]{:S(2)}) async-start(bf16[32,2,8192]{2,1,0:T(2,128)(2,1)} %reshape.116), calls=%async_computation.2 | async-start | bytes 2097152 | tf_op jit(solution)/shard_map/all_to_all | solution.py:95
  144.8 10.4 %all-to-all-start.6 = ((s32[16,4,128]{2,0,1:T(8,128)}), s32[16,4,128]{2,0,1:T(8,128)S(1)}, u32[]{:S(2)}, u32[]{:S(2)}) async-start(s32[16,4,128]{2,0,1:T(8,128)} %copy.85), calls=%async_computation.6 | async-start | bytes 65536 | tf_op jit(solution)/shard_map/all_to_all | solution.py:110
  155.1 34.5 %copy-start.20 = (s32[16,4,128]{2,0,1:T(8,128)}, s32[16,4,128]{2,0,1:T(8,128)S(1)}, u32[]{:S(2)}) copy-start(s32[16,4,128]{2,0,1:T(8,128)S(1)} %all-to-all-done.6) | copy-start | bytes 98308
  155.1 31.0 %all-to-all-start.3 = ((bf16[4,2,65536]{2,1,0:T(2,128)(2,1)}), bf16[4,2,65536]{2,1,0:T(2,128)(2,1)S(1)}, u32[]{:S(2)}, u32[]{:S(2)}) async-start(bf16[4,2,65536]{2,1,0:T(2,128)(2,1)} %reshape.118), calls=%async_computation.3 | async-start | bytes 2097152 | tf_op jit(solution)/shard_map/all_to_all | solution.py:106
  186.2 12.5 %all-to-all-start.4 = ((s32[16,4,128]{2,0,1:T(8,128)}), s32[16,4,128]{2,0,1:T(8,128)S(1)}, u32[]{:S(2)}, u32[]{:S(2)}) async-start(s32[16,4,128]{2,0,1:T(8,128)} %copy_bitcast_fusion.1), calls=%async_computation.4 | async-start | bytes 65536 | tf_op jit(solution)/shard_map/all_to_all | solution.py:107
  198.7 10.5 %all-to-all-start.8 = ((s32[16,4,128]{2,0,1:T(8,128)}), s32[16,4,128]{2,0,1:T(8,128)S(1)}, u32[]{:S(2)}, u32[]{:S(2)}) async-start(s32[16,4,128]{2,0,1:T(8,128)} %copy.88), calls=%async_computation.8 | async-start | bytes 65536 | tf_op jit(solution)/shard_map/all_to_all | solution.py:109
  203.6 192.5 %all-reduce.4.cloned.1.call-start = ((), (), s32[]{:S(2)}) async-start(), calls=%async_computation.9 | async-start | bytes 1572864 | tf_op jit(solution)/shard_map/psum | solution.py:145
  267.0 4.3 %copy-start.23 = (f32[128]{0:T(128)S(1)}, f32[128]{0:T(128)}, u32[]{:S(2)}) copy-start(f32[128]{0:T(128)} %get-tuple-element.123) | copy-start | bytes 1540
  267.0 4.3 %copy-start.26 = (f32[128]{0:T(128)S(1)}, f32[128]{0:T(128)}, u32[]{:S(2)}) copy-start(f32[128]{0:T(128)} %get-tuple-element.122) | copy-start | bytes 1540
  (61 other events, 101.1 us)
Sparse Core Ops, SparseCore 0:
  267.8 128.1 all-reduce.3
where the time goes:
time: 411 us; the launch traced here: 409 us
  waiting for transfers between devices  166 us (40%)
  matrix products  83.7 us (20%)
  starting transfers between devices  40.5 us (10%)
  blocking collectives  39.5 us (10%)
  local copies, waits for them, and re-layouts  37.7 us (9%)
  other arithmetic  24.3 us (6%)
  between operations  16.1 us (4%)
    psum x1, waiting for transfers between devices, shards(): lax.psum((loss_part, totals[0], totals[1], totals[2], totals[3], totals[4...  84.6 us
    psum x1, blocking collectives, shards(): lax.psum((loss_part, totals[0], totals[1], totals[2], totals[3], totals[4...  39.5 us
    all_to_all x1, waiting for transfers between devices, shards(): lax.all_to_all(half_back, 'col', split_axis=1, concat_axis=0, tiled=True)  25.3 us
    all_to_all x1, waiting for transfers between devices, shards(): lax.all_to_all(half_tile, 'col', split_axis=0, concat_axis=1, tiled=True)  24.8 us
    all_to_all x1, waiting for transfers between devices, shards(): lax.all_to_all(jnp.swapaxes(half_rows, 0, 1), ('row', 'col'), split_axis=...  23 us
    dot_general x4, matrix products, advance(): update = jnp.dot(hidden, out_weight, preferred_element_type=jnp.float32)  18.9 us
    dot_general x14, matrix products, inner(): lax.dot_general(left, right, (((0,), (0,)), ((), ())), preferred_element_...  17.7 us
    unnamed x33, local copies, waits for them, and re-layouts  16 us
  transfers between devices with their start and end apart: 10, of which 7 were waited for; matrix products, arithmetic and copies ran while one was open for 20% of the time, Pallas kernels for 0%

commit v1 on v0

--- a/solution.py
+++ b/solution.py
@@ -1,8 +1,11 @@
+import functools
 import math
 
 import jax
 import jax.numpy as jnp
 from jax import lax
+from jax.experimental import pallas as pl
+from jax.experimental.pallas import tpu as pltpu
 from jax.sharding import PartitionSpec as P
 
 EPSILON = 1e-05
@@ -74,6 +77,163 @@
     return (weights_mask[..., None] * (soft_probs - one_hot) / tokens).astype(jnp.bfloat16)
 
 
+def flip_bit(axis, bit):
+    place = lax.axis_index(axis)
+    mine = lax.rem(lax.div(place, bit), 2)
+    return mine, place + bit - 2 * bit * mine
+
+
+def total_kernel(bits, parts, shapes, *refs):
+    count = len(shapes)
+    ins, outs = refs[:count], refs[count : 2 * count]
+    acc, full, send_sem, recv_sem = refs[2 * count : 2 * count + 4]
+    landing = refs[2 * count + 4 :]
+    steps = len(bits)
+    barrier = pltpu.get_barrier_semaphore()
+    sides = []
+    for axis, bit in bits:
+        mine, partner = flip_bit(axis, bit)
+        sides.append((mine, {axis: partner}))
+        pl.semaphore_signal(
+            barrier, inc=1, device_id={axis: partner}, device_id_type=pl.DeviceIdType.MESH
+        )
+    row = 0
+    for ref, shape in zip(ins, shapes):
+        for left in range(0, shape[1], 128):
+            wide = min(128, shape[1] - left)
+            acc[row : row + shape[0], :wide] = ref[:, left : left + wide]
+            if wide < 128:
+                acc[row : row + shape[0], wide:] = jnp.zeros((shape[0], 128 - wide), jnp.float32)
+            row += shape[0]
+    if row < acc.shape[0]:
+        acc[row:, :] = jnp.zeros((acc.shape[0] - row, 128), jnp.float32)
+    pl.semaphore_wait(barrier, steps)
+
+    def push(part, slot, source, target, device):
+        return pltpu.make_async_remote_copy(
+            src_ref=source,
+            dst_ref=target,
+            send_sem=send_sem.at[part, slot],
+            recv_sem=recv_sem.at[part, slot],
+            device_id=device,
+            device_id_type=pl.DeviceIdType.MESH,
+        )
+
+    spots = [(base, size) for base, size, order in parts]
+    trail = [[] for part in parts]
+    for step in range(steps):
+        moves = []
+        for index, (base, size, order) in enumerate(parts):
+            mine, device = sides[order[step]]
+            start, length = spots[index]
+            land = landing[index * steps + step]
+            if step < steps - 1:
+                length //= 2
+                keep = pl.multiple_of(start + mine * length, 8)
+                give = pl.multiple_of(start + (1 - mine) * length, 8)
+                trail[index].append((keep, length, order[step]))
+            else:
+                keep = give = start
+            copy = push(index, step, acc.at[pl.ds(give, length)], land, device)
+            copy.start()
+            moves.append((copy, keep, length, land))
+            spots[index] = (keep, length)
+        for copy, keep, length, land in moves:
+            copy.wait()
+            into = acc if step < steps - 1 else full
+            into[pl.ds(keep, length), :] = acc[pl.ds(keep, length), :] + land[...]
+    for step in range(steps - 2, -1, -1):
+        moves = []
+        for index, (base, size, order) in enumerate(parts):
+            keep, length, which = trail[index][step]
+            spot = full.at[pl.ds(keep, length)]
+            copy = push(index, 2 * steps - 2 - step, spot, spot, sides[which][1])
+            copy.start()
+            moves.append(copy)
+        for copy in moves:
+            copy.wait()
+    row = 0
+    for ref, shape in zip(outs, shapes):
+        for left in range(0, shape[1], 128):
+            wide = min(128, shape[1] - left)
+            ref[:, left : left + wide] = full[row : row + shape[0], :wide]
+            row += shape[0]
+
+
+def total(arrays):
+    bits = []
+    for axis in ("row", "col"):
+        size, bit = lax.axis_size(axis), 1
+        if size & (size - 1):
+            return lax.psum(arrays, ("row", "col"))
+        while bit < size:
+            bits.append((axis, bit))
+            bit *= 2
+    if len(bits) < 2:
+        return lax.psum(arrays, ("row", "col"))
+    shapes = tuple(array.shape for array in arrays)
+    rows = sum(shape[0] * (-(-shape[1] // 128)) for shape in shapes)
+    steps = len(bits)
+    grain = 8 * 2 ** (steps - 1)
+    grains = -(-rows // grain)
+    inner_bits = list(range(1, steps - 1))
+    turns = max(1, min(3, len(inner_bits), grains))
+    parts, base = [], 0
+    for turn in range(turns):
+        size = grain * (grains // turns + (turn < grains % turns))
+        order = [0] + inner_bits[turn:] + inner_bits[:turn] + [steps - 1]
+        parts.append((base, size, order))
+        base += size
+    landing = []
+    for base_at, size, order in parts:
+        for step in range(steps):
+            landing.append(
+                pltpu.VMEM((size >> min(step + 1, steps - 1), 128), jnp.float32)
+            )
+    vmem = pl.BlockSpec(memory_space=pltpu.VMEM)
+    return pl.pallas_call(
+        functools.partial(total_kernel, bits, parts, shapes),
+        out_shape=[jax.ShapeDtypeStruct(shape, jnp.float32) for shape in shapes],
+        in_specs=[vmem] * len(shapes),
+        out_specs=[vmem] * len(shapes),
+        scratch_shapes=[
+            pltpu.VMEM((base, 128), jnp.float32),
+            pltpu.VMEM((base, 128), jnp.float32),
+            pltpu.SemaphoreType.DMA((turns, 2 * steps - 1)),
+            pltpu.SemaphoreType.DMA((turns, 2 * steps - 1)),
+        ]
+        + landing,
+        compiler_params=pltpu.CompilerParams(
+            collective_id=0, has_side_effects=True, vmem_limit_bytes=32 * 1024 * 1024
+        ),
+        name="total",
+    )(*arrays)
+
+
+def mirror(half_tile):
+    across, down = lax.axis_size("row"), lax.axis_size("col")
+    fold = across // down
+    edge, bins = half_tile.shape[0], half_tile.shape[2]
+    place, column = lax.axis_index("row"), lax.axis_index("col")
+    flipped = jnp.zeros_like(half_tile)
+    for turn in range(fold):
+        sub = lax.rem(place + turn, fold)
+        block = lax.dynamic_slice(half_tile, (0, sub * edge, 0), (edge, edge, bins))
+        packed = jnp.concatenate([block[: edge // 2], block[edge // 2 :]], axis=-1)
+        pairs = [
+            (r * down + c, (c * fold + (r + turn) % fold) * down + r // fold)
+            for r in range(across)
+            for c in range(down)
+        ]
+        came = lax.ppermute(packed, ("row", "col"), pairs)
+        whole = jnp.concatenate([came[..., :bins], came[..., bins:]], axis=0)
+        spot = lax.rem(place + turn * (fold - 1), fold)
+        flipped = lax.dynamic_update_slice(
+            flipped, jnp.swapaxes(whole, 0, 1), (0, spot * edge, 0)
+        )
+    return flipped
+
+
 def shards(
     pair, ln_gain, ln_bias, gate_weight, up_weight, out_weight, head_weight, targets, pair_mask
 ):
@@ -90,25 +250,14 @@
     half_tile = jnp.dot(pair_out, head_weight, preferred_element_type=jnp.float32).astype(
         jnp.bfloat16
     )
-    half_rows = lax.all_to_all(half_tile, "col", split_axis=0, concat_axis=1, tiled=True)
-    half_back, target_back, mask_back = (
-        lax.all_to_all(
-            jnp.swapaxes(half_rows, 0, 1), ("row", "col"), split_axis=0, concat_axis=1, tiled=True
-        ),
-        lax.all_to_all(
-            jnp.swapaxes(targets, 0, 1), ("row", "col"), split_axis=0, concat_axis=1, tiled=True
-        ),
-        lax.all_to_all(
-            jnp.swapaxes(pair_mask, 0, 1), ("row", "col"), split_axis=0, concat_axis=1, tiled=True
-        ),
-    )
-    half_flip, target_tile, mask_tile, target_turn, mask_turn = (
-        lax.all_to_all(half_back, "col", split_axis=1, concat_axis=0, tiled=True),
-        lax.all_to_all(targets, "col", split_axis=1, concat_axis=0, tiled=True),
-        lax.all_to_all(pair_mask, "col", split_axis=1, concat_axis=0, tiled=True),
-        lax.all_to_all(target_back, "col", split_axis=1, concat_axis=0, tiled=True),
-        lax.all_to_all(mask_back, "col", split_axis=1, concat_axis=0, tiled=True),
-    )
+    half_flip = mirror(half_tile)
+    code = jnp.where(pair_mask > 0, targets, -1)
+    codes = lax.all_gather(code, ("row", "col"), axis=0, tiled=True)
+    top, side = lax.axis_index("row") * rows_tile, lax.axis_index("col") * cols_tile
+    target_tile = lax.dynamic_slice(codes, (top, side), (rows_tile, cols_tile))
+    target_turn = lax.dynamic_slice(codes, (side, top), (cols_tile, rows_tile)).T
+    mask_tile = (target_tile >= 0).astype(jnp.int32)
+    mask_turn = (target_turn >= 0).astype(jnp.int32)
     logits = half_tile.astype(jnp.float32) + half_flip.astype(jnp.float32)
     loss_part, soft_probs = loss_terms(logits, target_tile, mask_tile)
     tile_grad = grad_from(soft_probs, target_tile, mask_tile, tokens)
@@ -142,12 +291,17 @@
         )
 
     totals, unused = lax.scan(backward_one, start, (blocks, grad_blocks))
-    summed = lax.psum(
-        (loss_part, totals[0], totals[1], totals[2], totals[3], totals[4], grad_head),
-        ("row", "col"),
-    )
-    loss = summed[0] / (tokens * tokens)
-    return (pair_out, loss, summed[1], summed[2], summed[3], summed[4], summed[5], summed[6])
+    few = jnp.concatenate(
+        [
+            totals[0][None],
+            totals[1][None],
+            jnp.broadcast_to(loss_part, (1, width)),
+            jnp.zeros((5, width), jnp.float32),
+        ]
+    )
+    gate_sum, up_sum, out_sum, head_sum, few = total([totals[2], totals[3], totals[4], grad_head, few])
+    loss = few[2, 0] / (tokens * tokens)
+    return (pair_out, loss, few[0], few[1], gate_sum, up_sum, out_sum, head_sum)
 
 
 def solution(mesh):

time: 411 us -> 281 us (0.68)
  waiting for transfers between devices: 166 us -> 0.04 us
  Pallas kernels: 0 us -> 93.4 us
  blocking collectives: 39.5 us -> 0 us
  starting transfers between devices: 40.5 us -> 2.17 us
  local copies, waits for them, and re-layouts: 37.7 us -> 52.4 us
    pallas_call x0 -> x1, Pallas kernels: none -> 93.4 us  [total(): pl.pallas_call(functools.partial(total_kernel, bits, parts, shapes), out_...]
    psum x1 -> x0, waiting for transfers between devices: 84.6 us -> none  [shards(): lax.psum((loss_part, totals[0], totals[1], totals[2], totals[3], totals[4...]
    all_to_all x9 -> x0, waiting for transfers between devices: 81.3 us -> none  [the longest x1 25.3 us: shards(): lax.all_to_all(half_back, 'col', split_axis=1, concat_axis=0, tiled=True)]
    all_to_all x9 -> x0, starting transfers between devices: 40.5 us -> none  [the longest x1 6.32 us: shards(): lax.all_to_all(pair_mask, 'col', split_axis=1, concat_axis=0, tiled=True)]
    psum x1 -> x0, blocking collectives: 39.5 us -> none  [shards(): lax.psum((loss_part, totals[0], totals[1], totals[2], totals[3], totals[4...]
    dynamic_update_slice x0 -> x2, local copies, waits for them, and re-layouts: none -> 25.1 us  [mirror(): lax.dynamic_update_slice(flipped, jnp.swapaxes(whole, 0, 1), (0, spot * e...]
    all_to_all x14 -> x0, local copies, waits for them, and re-layouts: 9.4 us -> none  [the longest x2 1.89 us: shards(): lax.all_to_all(jnp.swapaxes(half_rows, 0, 1), ('row', 'col'), split_axis=...]
    transpose x0 -> x2, other arithmetic: none -> 5.57 us  [mirror(): jnp.swapaxes(whole, 0, 1)]
  transfers between devices with their start and end apart: 10 -> 3, of which waited for: 7 -> 0; matrix products, arithmetic and copies ran while one was open for 20% -> 34% of each run, Pallas kernels for 0% -> 0%
where the time goes in v1:
time: 281 us; the launch traced here: 279 us
  Pallas kernels  93.4 us (33%)
  matrix products  85.6 us (30%)
  local copies, waits for them, and re-layouts  52.4 us (19%)
  other arithmetic  28.1 us (10%)
  between operations  16 us (6%)
    pallas_call x1, Pallas kernels, total(): pl.pallas_call(functools.partial(total_kernel, bits, parts, shapes), out_...  93.4 us
    dynamic_update_slice x2, local copies, waits for them, and re-layouts, mirror(): lax.dynamic_update_slice(flipped, jnp.swapaxes(whole, 0, 1), (0, spot * e...  25.1 us
    dot_general x4, matrix products, advance(): update = jnp.dot(hidden, out_weight, preferred_element_type=jnp.float32)  18.9 us
    dot_general x4, matrix products, advance(): gate_pre = jnp.dot(normed, gate_weight, preferred_element_type=jnp.float32)  15.9 us
    dot_general x14, matrix products, inner(): lax.dot_general(left, right, (((0,), (0,)), ((), ())), preferred_element_...  15.5 us
    unnamed x27, local copies, waits for them, and re-layouts  11.1 us
    reduce_sum x8, other arithmetic, normalize(): variance = jnp.mean(centered * centered, axis=-1, keepdims=True)  9.24 us
    dot_general x4, matrix products, retreat(): jnp.dot(grad_rows, out_weight.T, preferred_element_type=jnp.float32)  8.58 us
  transfers between devices with their start and end apart: 3, of which 0 were waited for; matrix products, arithmetic and copies ran while one was open for 34% of the time, Pallas kernels for 0%

profile of v1, /device:TPU:0, one launch (start us, length us, event | category | flops | bytes accessed | tf_op | source)
XLA Modules:
  0.0 279.3 jit_solution(6117539364025847219)
XLA Ops:
  8.7 47.0 %while.29 = (s32[]{:T(128)}, bf16[4,2048,128]{2,1,0:T(8,128)(2,1)}, bf16[4,2048,128]{2,1,0:T(8,128)(2,1)}, f32[128]{0:T(128)}, f32[128]{0:T(128)}, /*index=5*/bf...) while((s32[]{:T(128)}, bf16[4,2048,128]{2,1,0:T(8,128)(2,1)}, ...), condition=%wide.region_3.4_spmd, body=%wide.region_0.3_spmd.sunk | while | flops 817104896 | bytes 21462268 | solution.py:249
  9.9 1.7 fusion.126
  11.7 4.0 %fusion.127 = f32[2048,512]{1,0:T(8,128)} fusion(bf16[128,512]{1,0:T(8,128)(2,1)} %get-tuple-element.449, f32[128]{0:T(128)} %get-tuple-element.448, f32[128]{0:T(128)} %get-tuple-element.447, f32[2048]{0:T(1024)S(1)} %add_rsqrt_fusion.4, f32[2048]{0:T(1024)S(1)} %broadcast_multiply_fusion.4, bf16[4,2048,128]{2,1,0:T(8,128)(2,1)} %get-tuple-element.446, ...), kind=kOutput, calls=%fused_computation.14.clone.1 | convolution fusion | flops 270008320 | bytes 4867076 | tf_op jit(solution)/shard_map/while/body/eval_jaxpr/dot_general | solution.py:31
  15.7 4.7 %fusion.128 = bf16[4,2048,128]{2,1,0:T(8,128)(2,1)} fusion(bf16[4,2048,128]{2,1,0:T(8,128)(2,1)} %get-tuple-element.436, s32[]{:T(128)S(6)} %copy.98, bf16[512,128]{1,0:T(8,128)(2,1)S(1)} %copy-done.26, f32[2048,512]{1,0:T(8,128)} %fusion.127, bf16[128,512]{1,0:T(8,128)(2,1)S(1)} %copy-done.10, f32[128]{0:T(128)S(1)} %copy-done.15, ...), kind=kOutput, calls=%fused_computation.4.clone.1 | convolution fusion | flops 545521664 | bytes 6047744 | tf_op jit(solution)/shard_map/while/body/eval_jaxpr/dot_general | solution.py:34
  21.7 1.7 fusion.126
  23.4 4.0 %fusion.127 = f32[2048,512]{1,0:T(8,128)} fusion(bf16[128,512]{1,0:T(8,128)(2,1)} %get-tuple-element.449, f32[128]{0:T(128)} %get-tuple-element.448, f32[128]{0:T(128)} %get-tuple-element.447, f32[2048]{0:T(1024)S(1)} %add_rsqrt_fusion.4, f32[2048]{0:T(1024)S(1)} %broadcast_multiply_fusion.4, bf16[4,2048,128]{2,1,0:T(8,128)(2,1)} %get-tuple-element.446, ...), kind=kOutput, calls=%fused_computation.14.clone.1 | convolution fusion | flops 270008320 | bytes 4867076 | tf_op jit(solution)/shard_map/while/body/eval_jaxpr/dot_general | solution.py:31
  27.4 4.7 %fusion.128 = bf16[4,2048,128]{2,1,0:T(8,128)(2,1)} fusion(bf16[4,2048,128]{2,1,0:T(8,128)(2,1)} %get-tuple-element.436, s32[]{:T(128)S(6)} %copy.98, bf16[512,128]{1,0:T(8,128)(2,1)S(1)} %copy-done.26, f32[2048,512]{1,0:T(8,128)} %fusion.127, bf16[128,512]{1,0:T(8,128)(2,1)S(1)} %copy-done.10, f32[128]{0:T(128)S(1)} %copy-done.15, ...), kind=kOutput, calls=%fused_computation.4.clone.1 | convolution fusion | flops 545521664 | bytes 6047744 | tf_op jit(solution)/shard_map/while/body/eval_jaxpr/dot_general | solution.py:34
  33.4 1.7 fusion.126
  35.2 4.0 %fusion.127 = f32[2048,512]{1,0:T(8,128)} fusion(bf16[128,512]{1,0:T(8,128)(2,1)} %get-tuple-element.449, f32[128]{0:T(128)} %get-tuple-element.448, f32[128]{0:T(128)} %get-tuple-element.447, f32[2048]{0:T(1024)S(1)} %add_rsqrt_fusion.4, f32[2048]{0:T(1024)S(1)} %broadcast_multiply_fusion.4, bf16[4,2048,128]{2,1,0:T(8,128)(2,1)} %get-tuple-element.446, ...), kind=kOutput, calls=%fused_computation.14.clone.1 | convolution fusion | flops 270008320 | bytes 4867076 | tf_op jit(solution)/shard_map/while/body/eval_jaxpr/dot_general | solution.py:31
  39.2 4.7 %fusion.128 = bf16[4,2048,128]{2,1,0:T(8,128)(2,1)} fusion(bf16[4,2048,128]{2,1,0:T(8,128)(2,1)} %get-tuple-element.436, s32[]{:T(128)S(6)} %copy.98, bf16[512,128]{1,0:T(8,128)(2,1)S(1)} %copy-done.26, f32[2048,512]{1,0:T(8,128)} %fusion.127, bf16[128,512]{1,0:T(8,128)(2,1)S(1)} %copy-done.10, f32[128]{0:T(128)S(1)} %copy-done.15, ...), kind=kOutput, calls=%fused_computation.4.clone.1 | convolution fusion | flops 545521664 | bytes 6047744 | tf_op jit(solution)/shard_map/while/body/eval_jaxpr/dot_general | solution.py:34
  45.2 1.7 fusion.126
  47.0 4.0 %fusion.127 = f32[2048,512]{1,0:T(8,128)} fusion(bf16[128,512]{1,0:T(8,128)(2,1)} %get-tuple-element.449, f32[128]{0:T(128)} %get-tuple-element.448, f32[128]{0:T(128)} %get-tuple-element.447, f32[2048]{0:T(1024)S(1)} %add_rsqrt_fusion.4, f32[2048]{0:T(1024)S(1)} %broadcast_multiply_fusion.4, bf16[4,2048,128]{2,1,0:T(8,128)(2,1)} %get-tuple-element.446, ...), kind=kOutput, calls=%fused_computation.14.clone.1 | convolution fusion | flops 270008320 | bytes 4867076 | tf_op jit(solution)/shard_map/while/body/eval_jaxpr/dot_general | solution.py:31
  50.9 4.7 %fusion.128 = bf16[4,2048,128]{2,1,0:T(8,128)(2,1)} fusion(bf16[4,2048,128]{2,1,0:T(8,128)(2,1)} %get-tuple-element.436, s32[]{:T(128)S(6)} %copy.98, bf16[512,128]{1,0:T(8,128)(2,1)S(1)} %copy-done.26, f32[2048,512]{1,0:T(8,128)} %fusion.127, bf16[128,512]{1,0:T(8,128)(2,1)S(1)} %copy-done.10, f32[128]{0:T(128)S(1)} %copy-done.15, ...), kind=kOutput, calls=%fused_computation.4.clone.1 | convolution fusion | flops 545521664 | bytes 6047744 | tf_op jit(solution)/shard_map/while/body/eval_jaxpr/dot_general | solution.py:34
  55.7 2.4 convolution_convert_fusion
  63.9 1.7 collective-permute-start
  67.2 1.7 copy.82
  68.9 1.7 copy.83
  71.8 1.7 copy.80
  73.5 2.7 copy.81
  76.2 2.8 maximum_bitcast_fusion
  79.2 9.6 %dynamic_update_slice.10 = bf16[64,128,64]{1,2,0:T(8,128)(2,1)S(1)} dynamic-update-slice(bf16[64,128,64]{1,2,0:T(8,128)(2,1)S(1)} %broadcast_in_dim.33, bf16[64,64,64]{1,2,0:T(8,128)(2,1)} %maximum_bitcast_fusion, s32[]{:T(128)} %constant.70.clone.1, s32[]{:T(128)S(6)} %select_n.23, s32[]{:T(128)} %constant.70.clone.1) | dynamic-update-slice | bytes 1048580 | tf_op jit(solution)/shard_map/dynamic_update_slice | solution.py:231
  88.9 2.8 maximum_bitcast_fusion.1
  91.7 15.4 %dynamic_update_slice.11 = bf16[64,128,64]{1,2,0:T(8,128)(2,1)S(1)} dynamic-update-slice(bf16[64,128,64]{1,2,0:T(8,128)(2,1)S(1)} %dynamic_update_slice.10, bf16[64,64,64]{1,2,0:T(8,128)(2,1)} %maximum_bitcast_fusion.1, s32[]{:T(128)} %constant.70.clone.1, s32[]{:T(128)S(6)} %select_n.24, s32[]{:T(128)} %constant.70.clone.1) | dynamic-update-slice | bytes 1048580 | tf_op jit(solution)/shard_map/dynamic_update_slice | solution.py:231
  111.7 3.2 %fusion.68 = f32[64,128,128]{2,1,0:T(8,128)} fusion(bf16[128,64]{0,1:T(8,128)(2,1)S(1)} %copy-done, bf16[64,128,64]{1,2,0:T(8,128)(2,1)S(1)} %dynamic_update_slice.11, bf16[64,128,64]{1,2,0:T(8,128)(2,1)S(1)} %convolution_convert_fusion, s32[64,128]{1,0:T(8,128)S(1)} %get-tuple-element.266, f32[64,128]{1,0:T(8,128)S(1)} %get-tuple-element.282, ...), kind=kOutput, calls=%fused_computation.92 | convolution fusion | flops 139460608 | bytes 6406144 | tf_op jit(solution)/shard_map/dot_general | solution.py:272
  117.7 5.6 %add_convert_fusion = bf16[64,128,128]{2,1,0:T(8,128)(2,1)} fusion(f32[64,128,128]{2,1,0:T(8,128)} %fusion.68, bf16[128,64]{0,1:T(8,128)(2,1)S(1)} %copy-done, bf16[64,128,64]{1,2,0:T(8,128)(2,1)} %copy-done.4, bf16[64,128,64]{1,2,0:T(8,128)(2,1)S(1)} %convolution_convert_fusion, s32[64,128]{1,0:T(8,128)S(1)} %bitcast.161, f32[64,128]{1,0:T(8,128)} %copy-done.17, ...), kind=kOutput, calls=%fused_computation.67 | convolution fusion | flops 141557760 | bytes 8503296 | tf_op jit(solution)/shard_map/dot_general | solution.py:273
  123.3 49.3 %while.30 = (s32[]{:T(128)}, f32[128]{0:T(128)}, f32[128]{0:T(128)}, f32[128,512]{1,0:T(8,128)}, f32[128,512]{1,0:T(8,128)}, /*index=5*/f32[512,128]{1,0:T(8,128...) while((s32[]{:T(128)}, f32[128]{0:T(128)}, ...), condition=%wide.region_10.11_spmd.clone, body=%wide.region_5.0_spmd.clone.sunk | while | flops 2177501440 | bytes 62157384 | solution.py:293
  128.9 2.1 multiply_convert_fusion.14
  141.2 2.1 multiply_convert_fusion.14
  149.0 1.5 fusion.145
  153.5 2.1 multiply_convert_fusion.14
  165.7 2.1 multiply_convert_fusion.14
  173.4 93.4 %total.1 = (f32[128,512]{1,0:T(8,128)S(1)}, f32[128,512]{1,0:T(8,128)S(1)}, f32[512,128]{1,0:T(8,128)S(1)}, f32[128,64]{1,0:T(8,128)S(1)}, f32[8,128]{1,0:T(8,128)S(1)}) custom-call(f32[128,512]{1,0:T(8,128)} %get-tuple-element.127.refs_0_, f32[128,512]{1,0:T(8,128)} %get-tuple-element.128.refs_1_, f32[512,128]{1,0:T(8,128)} %get-tuple-element.129.refs_2_, ...), custom_call_target="tpu_custom_call" | custom-call | tf_op jit(solution)/shard_map/total/pallas_call | solution.py:194
  (269 shorter events, 65.4 us)
Async XLA Ops:
  7.2 48.5 %copy-start = (bf16[128,64]{0,1:T(8,128)(2,1)S(1)}, bf16[128,64]{0,1:T(8,128)(2,1)}, u32[]{:S(2)}) copy-start(bf16[128,64]{0,1:T(8,128)(2,1)} %param.19) | copy-start | bytes 49156
  7.2 100.0 %all-gather.2.cloned.1.call-start = ((), (), s32[]{:S(2)}) async-start(), calls=%async_computation | async-start | bytes 1081344 | tf_op jit(solution)/shard_map/all_gather | solution.py:255
  11.6 4.0 %copy-start.1 = (bf16[4,2048,128]{2,1,0:T(8,128)(2,1)S(1)}, bf16[4,2048,128]{2,1,0:T(8,128)(2,1)}, u32[]{:S(2)}) copy-start(bf16[4,2048,128]{2,1,0:T(8,128)(2,1)} %get-tuple-element.446) | copy-start | bytes 6291460 | tf_op jit(solution)/shard_map/while
  11.6 4.0 %copy-start.10 = (bf16[128,512]{1,0:T(8,128)(2,1)S(1)}, bf16[128,512]{1,0:T(8,128)(2,1)}, u32[]{:S(2)}) copy-start(bf16[128,512]{1,0:T(8,128)(2,1)} %get-tuple-element.450) | copy-start | bytes 393220 | tf_op jit(solution)/shard_map/while
  11.7 4.0 %copy-start.13 = (f32[128]{0:T(128)S(1)}, f32[128]{0:T(128)}, u32[]{:S(2)}) copy-start(f32[128]{0:T(128)} %get-tuple-element.447) | copy-start | bytes 1540 | tf_op jit(solution)/shard_map/while
  11.7 4.0 %copy-start.15 = (f32[128]{0:T(128)S(1)}, f32[128]{0:T(128)}, u32[]{:S(2)}) copy-start(f32[128]{0:T(128)} %get-tuple-element.448) | copy-start | bytes 1540 | tf_op jit(solution)/shard_map/while
  11.7 4.0 %copy-start.26 = (bf16[512,128]{1,0:T(8,128)(2,1)S(1)}, bf16[512,128]{1,0:T(8,128)(2,1)}, u32[]{:S(2)}) copy-start(bf16[512,128]{1,0:T(8,128)(2,1)} %get-tuple-element.451) | copy-start | bytes 393220 | tf_op jit(solution)/shard_map/while
  23.4 4.0 %copy-start.1 = (bf16[4,2048,128]{2,1,0:T(8,128)(2,1)S(1)}, bf16[4,2048,128]{2,1,0:T(8,128)(2,1)}, u32[]{:S(2)}) copy-start(bf16[4,2048,128]{2,1,0:T(8,128)(2,1)} %get-tuple-element.446) | copy-start | bytes 6291460 | tf_op jit(solution)/shard_map/while
  23.4 4.0 %copy-start.10 = (bf16[128,512]{1,0:T(8,128)(2,1)S(1)}, bf16[128,512]{1,0:T(8,128)(2,1)}, u32[]{:S(2)}) copy-start(bf16[128,512]{1,0:T(8,128)(2,1)} %get-tuple-element.450) | copy-start | bytes 393220 | tf_op jit(solution)/shard_map/while
  23.4 4.0 %copy-start.13 = (f32[128]{0:T(128)S(1)}, f32[128]{0:T(128)}, u32[]{:S(2)}) copy-start(f32[128]{0:T(128)} %get-tuple-element.447) | copy-start | bytes 1540 | tf_op jit(solution)/shard_map/while
  23.4 4.0 %copy-start.15 = (f32[128]{0:T(128)S(1)}, f32[128]{0:T(128)}, u32[]{:S(2)}) copy-start(f32[128]{0:T(128)} %get-tuple-element.448) | copy-start | bytes 1540 | tf_op jit(solution)/shard_map/while
  23.4 4.0 %copy-start.26 = (bf16[512,128]{1,0:T(8,128)(2,1)S(1)}, bf16[512,128]{1,0:T(8,128)(2,1)}, u32[]{:S(2)}) copy-start(bf16[512,128]{1,0:T(8,128)(2,1)} %get-tuple-element.451) | copy-start | bytes 393220 | tf_op jit(solution)/shard_map/while
  35.1 4.0 %copy-start.1 = (bf16[4,2048,128]{2,1,0:T(8,128)(2,1)S(1)}, bf16[4,2048,128]{2,1,0:T(8,128)(2,1)}, u32[]{:S(2)}) copy-start(bf16[4,2048,128]{2,1,0:T(8,128)(2,1)} %get-tuple-element.446) | copy-start | bytes 6291460 | tf_op jit(solution)/shard_map/while
  35.1 4.0 %copy-start.10 = (bf16[128,512]{1,0:T(8,128)(2,1)S(1)}, bf16[128,512]{1,0:T(8,128)(2,1)}, u32[]{:S(2)}) copy-start(bf16[128,512]{1,0:T(8,128)(2,1)} %get-tuple-element.450) | copy-start | bytes 393220 | tf_op jit(solution)/shard_map/while
  35.1 4.0 %copy-start.13 = (f32[128]{0:T(128)S(1)}, f32[128]{0:T(128)}, u32[]{:S(2)}) copy-start(f32[128]{0:T(128)} %get-tuple-element.447) | copy-start | bytes 1540 | tf_op jit(solution)/shard_map/while
  35.2 4.0 %copy-start.15 = (f32[128]{0:T(128)S(1)}, f32[128]{0:T(128)}, u32[]{:S(2)}) copy-start(f32[128]{0:T(128)} %get-tuple-element.448) | copy-start | bytes 1540 | tf_op jit(solution)/shard_map/while
  35.2 4.0 %copy-start.26 = (bf16[512,128]{1,0:T(8,128)(2,1)S(1)}, bf16[512,128]{1,0:T(8,128)(2,1)}, u32[]{:S(2)}) copy-start(bf16[512,128]{1,0:T(8,128)(2,1)} %get-tuple-element.451) | copy-start | bytes 393220 | tf_op jit(solution)/shard_map/while
  46.9 4.0 %copy-start.1 = (bf16[4,2048,128]{2,1,0:T(8,128)(2,1)S(1)}, bf16[4,2048,128]{2,1,0:T(8,128)(2,1)}, u32[]{:S(2)}) copy-start(bf16[4,2048,128]{2,1,0:T(8,128)(2,1)} %get-tuple-element.446) | copy-start | bytes 6291460 | tf_op jit(solution)/shard_map/while
  46.9 4.0 %copy-start.10 = (bf16[128,512]{1,0:T(8,128)(2,1)S(1)}, bf16[128,512]{1,0:T(8,128)(2,1)}, u32[]{:S(2)}) copy-start(bf16[128,512]{1,0:T(8,128)(2,1)} %get-tuple-element.450) | copy-start | bytes 393220 | tf_op jit(solution)/shard_map/while
  46.9 4.0 %copy-start.13 = (f32[128]{0:T(128)S(1)}, f32[128]{0:T(128)}, u32[]{:S(2)}) copy-start(f32[128]{0:T(128)} %get-tuple-element.447) | copy-start | bytes 1540 | tf_op jit(solution)/shard_map/while
  46.9 4.0 %copy-start.15 = (f32[128]{0:T(128)S(1)}, f32[128]{0:T(128)}, u32[]{:S(2)}) copy-start(f32[128]{0:T(128)} %get-tuple-element.448) | copy-start | bytes 1540 | tf_op jit(solution)/shard_map/while
  46.9 4.0 %copy-start.26 = (bf16[512,128]{1,0:T(8,128)(2,1)S(1)}, bf16[512,128]{1,0:T(8,128)(2,1)}, u32[]{:S(2)}) copy-start(bf16[512,128]{1,0:T(8,128)(2,1)} %get-tuple-element.451) | copy-start | bytes 393220 | tf_op jit(solution)/shard_map/while
  61.0 5.2 %collective-permute-start.1 = (bf16[32,64,128]{2,1,0:T(8,128)(2,1)}, bf16[32,64,128]{2,1,0:T(8,128)(2,1)S(1)}, u32[]{:S(2)}, u32[]{:S(2)}) collective-permute-start(bf16[32,64,128]{2,1,0:T(8,128)(2,1)} %copy.72), channel_id=1, source_target_pairs={{0,4},{1,12},{2,20},{3,28},{4,0},{5,8},{6,16},{7,24},{8,5},{9,13},... | collective-permute-start | bytes 1572872 | tf_op jit(solution)/shard_map/ppermute | solution.py:228
  63.9 6.7 %collective-permute-start = (bf16[32,64,128]{2,1,0:T(8,128)(2,1)}, bf16[32,64,128]{2,1,0:T(8,128)(2,1)S(1)}, u32[]{:S(2)}, u32[]{:S(2)}) collective-permute-start(bf16[32,64,128]{2,1,0:T(8,128)(2,1)} %copy.69), channel_id=1, source_target_pairs={{0,0},{1,8},{2,16},{3,24},{4,4},{5,12},{6,20},{7,28},{8,1},{9,9},{... | collective-permute-start | bytes 1572872 | tf_op jit(solution)/shard_map/ppermute | solution.py:228
  107.1 7.8 %copy-start.4 = (bf16[64,128,64]{1,2,0:T(8,128)(2,1)}, bf16[64,128,64]{1,2,0:T(8,128)(2,1)S(1)}, u32[]{:S(2)}) copy-start(bf16[64,128,64]{1,2,0:T(8,128)(2,1)S(1)} %dynamic_update_slice.11) | copy-start | bytes 3145732
  109.0 5.9 %copy-start.17 = (f32[64,128]{1,0:T(8,128)}, f32[64,128]{1,0:T(8,128)S(1)}, u32[]{:S(2)}) copy-start(f32[64,128]{1,0:T(8,128)S(1)} %get-tuple-element.285) | copy-start | bytes 98308
  117.7 5.6 %copy-start.2 = (bf16[4,2048,128]{2,1,0:T(8,128)(2,1)S(1)}, bf16[4,2048,128]{2,1,0:T(8,128)(2,1)}, u32[]{:S(2)}) copy-start(bf16[4,2048,128]{2,1,0:T(8,128)(2,1)} %get-tuple-element.515) | copy-start | bytes 6291460
  117.7 5.6 %copy-start.3 = (bf16[128,512]{1,0:T(8,128)(2,1)S(1)}, bf16[128,512]{1,0:T(8,128)(2,1)}, u32[]{:S(2)}) copy-start(bf16[128,512]{1,0:T(8,128)(2,1)} %get-tuple-element.516) | copy-start | bytes 393220
  117.7 5.6 %copy-start.11 = (bf16[128,512]{1,0:T(8,128)(2,1)S(1)}, bf16[128,512]{1,0:T(8,128)(2,1)}, u32[]{:S(2)}) copy-start(bf16[128,512]{1,0:T(8,128)(2,1)} %get-tuple-element.517) | copy-start | bytes 393220
  123.3 49.4 %copy-start.24 = (f32[8]{0:T(128)S(1)}, f32[8]{0:T(128)}, u32[]{:S(2)}) copy-start(f32[8]{0:T(128)} %pad.3.clone) | copy-start | bytes 100
  123.3 49.4 %copy-start.25 = (f32[8]{0:T(128)S(1)}, f32[8]{0:T(128)}, u32[]{:S(2)}) copy-start(f32[8]{0:T(128)} %pad.2.clone) | copy-start | bytes 100
  153.4 2.2 copy-start.19
  (56 other events, 75.1 us)
Sparse Core Ops, SparseCore 0:
  11.6 56.4 all-gather.1

commit v2 on v1

--- a/solution.py
+++ b/solution.py
@@ -35,46 +35,32 @@
     return (rows_in.astype(jnp.float32) + update).astype(jnp.bfloat16)
 
 
-def retreat(totals, rows_in, grad_rows, ln_gain, ln_bias, gate_weight, up_weight, out_weight):
+def against(left, right):
+    return lax.dot_general(
+        left, right, (((1,), (1,)), ((), ())), preferred_element_type=jnp.float32
+    )
+
+
+def retreat(rows_in, grad_rows, ln_gain, ln_bias, gate_weight, up_weight, out_weight):
     unit_rows, normed = normalize(rows_in, ln_gain, ln_bias)
     gate_pre = jnp.dot(normed, gate_weight, preferred_element_type=jnp.float32)
     up_pre = jnp.dot(normed, up_weight, preferred_element_type=jnp.float32)
     squashed = jax.nn.sigmoid(gate_pre)
     silu_val = gate_pre * squashed
     hidden = (silu_val * up_pre).astype(jnp.bfloat16)
-    grad_hidden = jnp.dot(grad_rows, out_weight.T, preferred_element_type=jnp.float32)
+    grad_hidden = against(grad_rows, out_weight)
     grad_gate_pre = (grad_hidden * up_pre * squashed * (1.0 + gate_pre * (1.0 - squashed))).astype(
         jnp.bfloat16
     )
     grad_up_pre = (grad_hidden * silu_val).astype(jnp.bfloat16)
-    grad_normed = jnp.dot(
-        grad_gate_pre, gate_weight.T, preferred_element_type=jnp.float32
-    ) + jnp.dot(grad_up_pre, up_weight.T, preferred_element_type=jnp.float32)
-    sum_gain, sum_bias, sum_gate, sum_up, sum_out = totals
+    grad_normed = against(grad_gate_pre, gate_weight) + against(grad_up_pre, up_weight)
     return (
-        sum_gain + jnp.sum(grad_normed * unit_rows, axis=0),
-        sum_bias + jnp.sum(grad_normed, axis=0),
-        sum_gate + inner(normed, grad_gate_pre),
-        sum_up + inner(normed, grad_up_pre),
-        sum_out + inner(hidden, grad_rows),
-    )
-
-
-def loss_terms(logits, targets, pair_mask):
-    bins = logits.shape[-1]
-    one_hot = (targets[..., None] == jnp.arange(bins, dtype=jnp.int32)).astype(jnp.float32)
-    log_total = jnp.log(jnp.sum(jnp.exp(logits), axis=-1))
-    weights_mask = pair_mask.astype(jnp.float32)
-    loss_part = jnp.sum(weights_mask * (log_total - jnp.sum(logits * one_hot, axis=-1)))
-    soft_probs = jnp.exp(logits - log_total[..., None])
-    return (loss_part, soft_probs)
-
-
-def grad_from(soft_probs, targets, pair_mask, tokens):
-    bins = soft_probs.shape[-1]
-    one_hot = (targets[..., None] == jnp.arange(bins, dtype=jnp.int32)).astype(jnp.float32)
-    weights_mask = pair_mask.astype(jnp.float32)
-    return (weights_mask[..., None] * (soft_probs - one_hot) / tokens).astype(jnp.bfloat16)
+        jnp.sum(grad_normed * unit_rows, axis=0, keepdims=True),
+        jnp.sum(grad_normed, axis=0, keepdims=True),
+        inner(normed, grad_gate_pre),
+        inner(normed, grad_up_pre),
+        inner(grad_rows, hidden),
+    )
 
 
 def flip_bit(axis, bit):
@@ -210,96 +196,243 @@
     )(*arrays)
 
 
-def mirror(half_tile):
+def forward_kernel(
+    pair_ref, gain_ref, bias_ref, gate_ref, up_ref, out_ref, both_ref, *results
+):
+    rows_ref, packed_ref = results
+    shape = pair_ref.shape
+    rows_out = advance(
+        pair_ref[...].reshape(-1, shape[3]),
+        gain_ref[...],
+        bias_ref[...],
+        gate_ref[...],
+        up_ref[...],
+        out_ref[...],
+    )
+    rows_ref[...] = rows_out.reshape(shape)
+    middle = rows_out.shape[0] // 2
+    wide = jnp.concatenate([rows_out[:middle], rows_out[middle:]], axis=1)
+    packed = jnp.dot(wide, both_ref[...], preferred_element_type=jnp.float32)
+    packed_ref[...] = packed.astype(jnp.bfloat16).reshape(packed_ref.shape)
+
+
+def forward(piece, pieces, pair, gain, bias, gate_weight, up_weight, out_weight, head_weight):
+    rows_tile, cols_tile, width = pair.shape
+    bins = head_weight.shape[1]
+    deep = rows_tile // pieces
+    group = math.gcd(deep // 2, max(1, 512 // cols_tile))
+    empty = jnp.zeros_like(head_weight)
+    both = jnp.concatenate(
+        [
+            jnp.concatenate([head_weight, empty], axis=1),
+            jnp.concatenate([empty, head_weight], axis=1),
+        ]
+    )
+    def whole(array):
+        return pl.BlockSpec(array.shape, lambda step: (0, 0))
+
+    split = pair.reshape(2 * pieces, deep // 2, cols_tile, width)
+    weights = [gain[None], bias[None], gate_weight, up_weight, out_weight, both]
+    rows_out, packed = pl.pallas_call(
+        forward_kernel,
+        grid=(deep // 2 // group,),
+        out_shape=[
+            jax.ShapeDtypeStruct((2, deep // 2, cols_tile, width), jnp.bfloat16),
+            jax.ShapeDtypeStruct((deep // 2, cols_tile, 2 * bins), jnp.bfloat16),
+        ],
+        in_specs=[
+            pl.BlockSpec((2, group, cols_tile, width), lambda step: (piece, step, 0, 0))
+        ]
+        + [whole(array) for array in weights],
+        out_specs=[
+            pl.BlockSpec((2, group, cols_tile, width), lambda step: (0, step, 0, 0)),
+            pl.BlockSpec((group, cols_tile, 2 * bins), lambda step: (step, 0, 0)),
+        ],
+        compiler_params=pltpu.CompilerParams(vmem_limit_bytes=32 * 1024 * 1024),
+        cost_estimate=pl.CostEstimate(
+            flops=6 * deep * cols_tile * width * gate_weight.shape[1],
+            bytes_accessed=6 * deep * cols_tile * width,
+            transcendentals=deep * cols_tile * gate_weight.shape[1],
+        ),
+        name="forward",
+    )(split, *weights)
+    return (
+        rows_out.reshape(deep, cols_tile, width),
+        packed,
+    )
+
+
+def mirror(packed_part):
     across, down = lax.axis_size("row"), lax.axis_size("col")
     fold = across // down
-    edge, bins = half_tile.shape[0], half_tile.shape[2]
-    place, column = lax.axis_index("row"), lax.axis_index("col")
-    flipped = jnp.zeros_like(half_tile)
+    deep, cols_tile, bins = packed_part.shape
+    edge = cols_tile // fold
+    place = lax.axis_index("row")
+    came = []
     for turn in range(fold):
         sub = lax.rem(place + turn, fold)
-        block = lax.dynamic_slice(half_tile, (0, sub * edge, 0), (edge, edge, bins))
-        packed = jnp.concatenate([block[: edge // 2], block[edge // 2 :]], axis=-1)
+        packed = lax.dynamic_slice(packed_part, (0, sub * edge, 0), (deep, edge, bins))
         pairs = [
             (r * down + c, (c * fold + (r + turn) % fold) * down + r // fold)
             for r in range(across)
             for c in range(down)
         ]
-        came = lax.ppermute(packed, ("row", "col"), pairs)
-        whole = jnp.concatenate([came[..., :bins], came[..., bins:]], axis=0)
-        spot = lax.rem(place + turn * (fold - 1), fold)
-        flipped = lax.dynamic_update_slice(
-            flipped, jnp.swapaxes(whole, 0, 1), (0, spot * edge, 0)
-        )
-    return flipped
+        came.append(lax.ppermute(packed, ("row", "col"), pairs))
+    return came
+
+
+def ordered(came):
+    fold = len(came)
+    place = lax.axis_index("row")
+    stacked = jnp.stack(came)
+    return jnp.concatenate(
+        [
+            lax.dynamic_slice_in_dim(stacked, lax.rem(place + fold - sub, fold), 1)
+            for sub in range(fold)
+        ]
+    )
+
+
+def backward_kernel(tokens, *refs):
+    pair_ref, rows_ref, flip_ref, code_ref, turn_ref = refs[:5]
+    gain_ref, bias_ref, gate_ref, up_ref, out_ref, head_ref = refs[5:11]
+    before, after = refs[11:16], refs[16:21]
+
+    @pl.when((pl.program_id(0) == 0) & (pl.program_id(1) == 0))
+    def start():
+        for old, new in zip(before, after):
+            new[...] = old[...]
+
+    shape = pair_ref.shape
+    bins = head_ref.shape[1]
+    rows_in = pair_ref[...].reshape(-1, shape[3])
+    rows_out = rows_ref[...].reshape(-1, shape[3])
+    half = jnp.dot(rows_out, head_ref[...], preferred_element_type=jnp.float32)
+    half = half.astype(jnp.bfloat16).astype(jnp.float32)
+    packed = jnp.swapaxes(flip_ref[0].astype(jnp.float32), 0, 1)
+    flipped = jnp.concatenate([packed[..., :bins], packed[..., bins:]], axis=1)
+    logits = half.reshape(flipped.shape) + flipped
+    bin_at = lax.broadcasted_iota(jnp.int32, logits.shape, 2)
+    log_total = jnp.log(jnp.sum(jnp.exp(logits), axis=-1, keepdims=True))
+    soft_probs = jnp.exp(logits - log_total)
+
+    def split(ref):
+        codes = lax.broadcast_in_dim(ref[0], logits.shape, (0, 1))
+        hot = (codes == bin_at).astype(jnp.float32)
+        return hot, (codes >= 0).astype(jnp.float32)
+
+    hot, mask = split(code_ref)
+    hot_turn, mask_turn = split(turn_ref)
+    loss_rows = mask[..., :1] * (log_total - jnp.sum(logits * hot, axis=-1, keepdims=True))
+    tile_grad = (mask * (soft_probs - hot) / tokens).astype(jnp.bfloat16)
+    tile_flip = (mask_turn * (soft_probs - hot_turn) / tokens).astype(jnp.bfloat16)
+    both = jnp.concatenate([tile_grad.reshape(-1, bins), tile_flip.reshape(-1, bins)], axis=1)
+    head = head_ref[...]
+    grad_rows = against(both, jnp.concatenate([head, head], axis=1)).astype(jnp.bfloat16)
+    gain_sum, bias_sum, gate_sum, up_sum, out_sum = retreat(
+        rows_in, grad_rows, gain_ref[...], bias_ref[...], gate_ref[...], up_ref[...], out_ref[...]
+    )
+    after[0][...] += gate_sum
+    after[1][...] += up_sum
+    after[2][...] += out_sum
+    after[3][...] += inner(rows_out, both)
+    few = after[4]
+    few[0:1, :] += gain_sum
+    few[1:2, :] += bias_sum
+    few[2:3, :] += jnp.broadcast_to(jnp.sum(loss_rows), gain_sum.shape)
+
+
+def backward(
+    piece, pieces, tokens, totals, pair, pair_out, flips, codes, turns, weights
+):
+    rows_tile, cols_tile, width = pair.shape
+    fold = flips.shape[0]
+    deep = cols_tile // (fold * pieces)
+    group = math.gcd(rows_tile, max(8, 1024 // deep))
+
+    def whole(array):
+        return pl.BlockSpec(array.shape, lambda sub, step: (0, 0))
+
+    tile = pl.BlockSpec(
+        (group, 1, deep, width), lambda sub, step: (step, sub * pieces + piece, 0, 0)
+    )
+    code = pl.BlockSpec((1, group, deep), lambda sub, step: (sub * pieces + piece, step, 0))
+    flip = pl.BlockSpec(
+        (1, deep // 2, group, flips.shape[3]), lambda sub, step: (sub, 0, step, 0)
+    )
+    cut = (rows_tile, fold * pieces, deep, width)
+    return pl.pallas_call(
+        functools.partial(backward_kernel, tokens),
+        grid=(fold, rows_tile // group),
+        out_shape=[jax.ShapeDtypeStruct(array.shape, jnp.float32) for array in totals],
+        in_specs=[tile, tile, flip, code, code]
+        + [whole(array) for array in weights]
+        + [whole(array) for array in totals],
+        out_specs=[whole(array) for array in totals],
+        compiler_params=pltpu.CompilerParams(vmem_limit_bytes=48 * 1024 * 1024),
+        cost_estimate=pl.CostEstimate(
+            flops=16 * rows_tile * deep * fold * width * weights[2].shape[1],
+            bytes_accessed=8 * rows_tile * deep * fold * width,
+            transcendentals=rows_tile * deep * fold * weights[2].shape[1],
+        ),
+        name="backward",
+    )(pair.reshape(cut), pair_out.reshape(cut), flips, codes, turns, *weights, *totals)
 
 
 def shards(
     pair, ln_gain, ln_bias, gate_weight, up_weight, out_weight, head_weight, targets, pair_mask
 ):
     rows_tile, cols_tile, width = pair.shape
+    bins = head_weight.shape[1]
     tokens = cols_tile * lax.axis_size("col")
-    block_rows = math.gcd(rows_tile, max(1, 2048 // cols_tile))
-    count = rows_tile // block_rows
-    blocks = pair.reshape(count, block_rows * cols_tile, width)
-
-    def forward_one(rows_in):
-        return advance(rows_in, ln_gain, ln_bias, gate_weight, up_weight, out_weight)
-
-    pair_out = lax.map(forward_one, blocks).reshape(pair.shape)
-    half_tile = jnp.dot(pair_out, head_weight, preferred_element_type=jnp.float32).astype(
-        jnp.bfloat16
-    )
-    half_flip = mirror(half_tile)
+    fold = lax.axis_size("row") // lax.axis_size("col")
+    pieces = 2
+    deep = rows_tile // pieces
+
     code = jnp.where(pair_mask > 0, targets, -1)
     codes = lax.all_gather(code, ("row", "col"), axis=0, tiled=True)
     top, side = lax.axis_index("row") * rows_tile, lax.axis_index("col") * cols_tile
-    target_tile = lax.dynamic_slice(codes, (top, side), (rows_tile, cols_tile))
-    target_turn = lax.dynamic_slice(codes, (side, top), (cols_tile, rows_tile)).T
-    mask_tile = (target_tile >= 0).astype(jnp.int32)
-    mask_turn = (target_turn >= 0).astype(jnp.int32)
-    logits = half_tile.astype(jnp.float32) + half_flip.astype(jnp.float32)
-    loss_part, soft_probs = loss_terms(logits, target_tile, mask_tile)
-    tile_grad = grad_from(soft_probs, target_tile, mask_tile, tokens)
-    tile_flip = grad_from(soft_probs, target_turn, mask_turn, tokens)
-    bins = head_weight.shape[1]
-    flat_out = pair_out.reshape(-1, width)
-    grad_head = inner(flat_out, tile_grad.reshape(-1, bins)) + inner(
-        flat_out, tile_flip.reshape(-1, bins)
-    )
-    head_back = head_weight.T
-    grad_pair = (
-        jnp.dot(tile_grad, head_back, preferred_element_type=jnp.float32)
-        + jnp.dot(tile_flip, head_back, preferred_element_type=jnp.float32)
-    ).astype(jnp.bfloat16)
-    grad_blocks = grad_pair.reshape(count, block_rows * cols_tile, width)
+    code_tile = lax.dynamic_slice(codes, (top, side), (rows_tile, cols_tile))
+    code_turn = lax.dynamic_slice(codes, (side, top), (cols_tile, rows_tile)).T
+
+    outs, arrivals = [], []
+    for piece in range(pieces):
+        rows_out, packed = forward(
+            piece, pieces, pair, ln_gain, ln_bias, gate_weight, up_weight, out_weight, head_weight
+        )
+        outs.append(rows_out)
+        arrivals.append(mirror(packed))
+    pair_out = jnp.concatenate(outs)
+
+    def by_columns(array):
+        return jnp.swapaxes(array.reshape(rows_tile, fold * pieces, deep), 0, 1)
+
     hidden_width = gate_weight.shape[1]
-    start = (
-        jnp.zeros((width,), jnp.float32),
-        jnp.zeros((width,), jnp.float32),
+    totals = [
         jnp.zeros((width, hidden_width), jnp.float32),
         jnp.zeros((width, hidden_width), jnp.float32),
-        jnp.zeros((hidden_width, width), jnp.float32),
-    )
-
-    def backward_one(totals, inputs):
-        return (
-            retreat(
-                totals, inputs[0], inputs[1], ln_gain, ln_bias, gate_weight, up_weight, out_weight
-            ),
-            None,
+        jnp.zeros((width, hidden_width), jnp.float32),
+        jnp.zeros((width, 2 * bins), jnp.float32),
+        jnp.zeros((8, width), jnp.float32),
+    ]
+    weights = [ln_gain[None], ln_bias[None], gate_weight, up_weight, out_weight, head_weight]
+    codes_here, codes_turn = by_columns(code_tile), by_columns(code_turn)
+    for piece in range(pieces):
+        totals = backward(
+            piece,
+            pieces,
+            tokens,
+            totals,
+            pair,
+            pair_out,
+            ordered(arrivals[piece]),
+            codes_here,
+            codes_turn,
+            weights,
         )
-
-    totals, unused = lax.scan(backward_one, start, (blocks, grad_blocks))
-    few = jnp.concatenate(
-        [
-            totals[0][None],
-            totals[1][None],
-            jnp.broadcast_to(loss_part, (1, width)),
-            jnp.zeros((5, width), jnp.float32),
-        ]
-    )
-    gate_sum, up_sum, out_sum, head_sum, few = total([totals[2], totals[3], totals[4], grad_head, few])
+    gate_sum, up_sum, out_sum, head_sum, few = total(list(totals))
+    head_sum = head_sum[:, :bins] + head_sum[:, bins:]
+    out_sum = out_sum.T
     loss = few[2, 0] / (tokens * tokens)
     return (pair_out, loss, few[0], few[1], gate_sum, up_sum, out_sum, head_sum)
 

time: 281 us -> 201 us (0.72)
  matrix products: 85.6 us -> 0 us
  waiting for transfers between devices: 0.04 us -> 77.4 us
  local copies, waits for them, and re-layouts: 52.4 us -> 14.1 us
  other arithmetic: 28.1 us -> 6.26 us
  Pallas kernels: 93.4 us -> 83.1 us
    dot_general x45 -> x0, matrix products: 85.6 us -> none  [the longest x4 18.9 us: advance(): update = jnp.dot(hidden, out_weight, preferred_element_type=jnp.float32)]
    all_gather x1, waiting for transfers between devices: 0.02 us -> 77.3 us  [shards(): codes = lax.all_gather(code, ('row', 'col'), axis=0, tiled=True)]
    pallas_call x1, Pallas kernels: 93.4 us -> 27.9 us  [total(): pl.pallas_call(functools.partial(total_kernel, bits, parts, shapes), out_...]
    pallas_call x0 -> x4, Pallas kernels: none -> 55.3 us  [the longest x2 42.1 us: backward(): pl.pallas_call(functools.partial(backward_kernel, tokens), grid=(fold, ro...]
    dynamic_update_slice x2 -> x0, local copies, waits for them, and re-layouts: 25.1 us -> none  [mirror(): lax.dynamic_update_slice(flipped, jnp.swapaxes(whole, 0, 1), (0, spot * e...]
    reduce_sum x18 -> x0, other arithmetic: 16.6 us -> none  [the longest x8 9.24 us: normalize(): variance = jnp.mean(centered * centered, axis=-1, keepdims=True)]
    while x152 -> x0, local copies, waits for them, and re-layouts: 6.17 us -> none
    transpose x2 -> x0, other arithmetic: 5.57 us -> none  [mirror(): jnp.swapaxes(whole, 0, 1)]
  transfers between devices with their start and end apart: 3 -> 5, of which waited for: 0 -> 1; matrix products, arithmetic and copies ran while one was open for 34% -> 3% of each run, Pallas kernels for 0% -> 7%
where the time goes in v2:
time: 201 us; the launch traced here: 200 us
  Pallas kernels  83.1 us (41%)
  waiting for transfers between devices  77.4 us (39%)
  between operations  16.1 us (8%)
  local copies, waits for them, and re-layouts  14.1 us (7%)
  other arithmetic  6.26 us (3%)
  starting transfers between devices  3.38 us (2%)
    all_gather x1, waiting for transfers between devices, shards(): codes = lax.all_gather(code, ('row', 'col'), axis=0, tiled=True)  77.3 us
    pallas_call x2, Pallas kernels, backward(): pl.pallas_call(functools.partial(backward_kernel, tokens), grid=(fold, ro...  42.1 us
    pallas_call x1, Pallas kernels, total(): pl.pallas_call(functools.partial(total_kernel, bits, parts, shapes), out_...  27.9 us
    pallas_call x2, Pallas kernels, forward(): pl.pallas_call(forward_kernel, grid=(deep // 2 // group,), out_shape=[jax...  13.1 us
    unnamed x30, local copies, waits for them, and re-layouts  11.1 us
  transfers between devices with their start and end apart: 5, of which 1 were waited for; matrix products, arithmetic and copies ran while one was open for 3% of the time, Pallas kernels for 7%

profile of v2, /device:TPU:0, one launch (start us, length us, event | category | flops | bytes accessed | tf_op | source)
XLA Modules:
  0.0 200.3 jit_solution(3973157063589855531)
XLA Ops:
  7.2 1.4 compare_select_fusion
  8.6 0.8 copy.35.refs_10_
  9.6 1.6 copy-done
  11.2 0.9 copy-done.2
  12.1 0.9 copy-done.4
  13.0 0.9 copy-done.6
  13.9 0.7 copy-done.8
  14.5 0.7 copy-done.10
  15.2 6.6 %forward.3 = (bf16[2,16,128,128]{3,2,1,0:T(8,128)(2,1)S(1)}, bf16[16,128,128]{2,1,0:T(8,128)(2,1)S(1)}) custom-call(bf16[4,16,128,128]{3,2,1,0:T(8,128)(2,1)S(1)} %bitcast.33, f32[1,128]{1,0:T(1,128)S(1)} %bitcast.37, f32[1,128]{1,0:T(1,128)S(1)} %bitcast.41, bf16[128,512]{1,0:T(8,128)(2,1)S(1)} %copy-done.2, bf16[128,512]{1,0:T(8,128)(2,1)S(1)} %copy-done.4, ...), custom_call_target="tpu_custom_call" | custom-call | flops 1610612736 | bytes 3145728 | tf_op jit(solution)/shard_map/forward/pallas_call | solution.py:236
  21.8 0.5 collective-permute-start.1
  22.3 1.3 collective-permute-start
  23.7 6.6 %forward.2 = (bf16[2,16,128,128]{3,2,1,0:T(8,128)(2,1)S(1)}, bf16[16,128,128]{2,1,0:T(8,128)(2,1)S(1)}) custom-call(bf16[4,16,128,128]{3,2,1,0:T(8,128)(2,1)S(1)} %bitcast.34, f32[1,128]{1,0:T(1,128)S(1)} %bitcast.38, f32[1,128]{1,0:T(1,128)S(1)} %bitcast.42, bf16[128,512]{1,0:T(8,128)(2,1)S(1)} %copy-done.2, bf16[128,512]{1,0:T(8,128)(2,1)S(1)} %copy-done.4, ...), custom_call_target="tpu_custom_call" | custom-call | flops 1610612736 | bytes 3145728 | tf_op jit(solution)/shard_map/forward/pallas_call | solution.py:236
  30.3 0.1 collective-permute-start.3
  30.4 1.4 collective-permute-start.2
  31.8 1.5 pad_maximum_fusion.1.refs_1_
  33.3 1.5 pad_maximum_fusion
  34.9 1.6 fusion.1
  36.6 77.3 %all-gather.2.cloned.1.call-done = s32[512,512]{1,0:T(8,128)} async-done(((s32[16,512]{1,0:T(8,128)}), s32[512,512]{1,0:T(8,128)}) %all-gather.2.cloned.1.call-update) | async-done | bytes 1048592 | tf_op jit(solution)/shard_map/all_gather | solution.py:393
  113.9 0.8 dynamic_slice.34
  114.8 0.1 copy.38
  114.9 0.9 dynamic_slice.35
  115.8 0.1 copy.39
  116.0 1.6 copy-done.1
  117.6 21.1 %backward.2 = (f32[128,512]{1,0:T(8,128)S(1)}, f32[128,512]{1,0:T(8,128)S(1)}, f32[128,512]{1,0:T(8,128)S(1)}, f32[128,128]{1,0:T(8,128)S(1)}, f32[8,128]{1,0:T(8,128)S(1)}) custom-call(bf16[64,4,32,128]{3,2,1,0:T(8,128)(2,1)S(1)} %bitcast.35, bf16[64,4,32,128]{3,2,1,0:T(8,128)(2,1)} %pad_maximum_fusion.1.refs_1_, ...), custom_call_target="tpu_custom_call" | custom-call | flops 4294967296 | bytes 4194304 | tf_op jit(solution)/shard_map/backward/pallas_call | solution.py:364
  138.7 21.1 %backward.3 = (f32[128,512]{1,0:T(8,128)S(1)}, f32[128,512]{1,0:T(8,128)S(1)}, f32[128,512]{1,0:T(8,128)S(1)}, f32[128,128]{1,0:T(8,128)S(1)}, f32[8,128]{1,0:T(8,128)S(1)}) custom-call(bf16[64,4,32,128]{3,2,1,0:T(8,128)(2,1)S(1)} %bitcast.36, bf16[64,4,32,128]{3,2,1,0:T(8,128)(2,1)} %pad_maximum_fusion.1.refs_1_, ...), custom_call_target="tpu_custom_call" | custom-call | flops 4294967296 | bytes 4194304 | tf_op jit(solution)/shard_map/backward/pallas_call | solution.py:364
  159.8 27.9 %total.1 = (f32[128,512]{1,0:T(8,128)S(1)}, f32[128,512]{1,0:T(8,128)S(1)}, f32[128,512]{1,0:T(8,128)S(1)}, f32[128,128]{1,0:T(8,128)S(1)}, f32[8,128]{1,0:T(8,128)S(1)}) custom-call(f32[128,512]{1,0:T(8,128)S(1)} %get-tuple-element.36.refs_0_, f32[128,512]{1,0:T(8,128)S(1)} %get-tuple-element.37.refs_1_, f32[128,512]{1,0:T(8,128)S(1)} %get-tuple-element.38.refs_2_, ...), custom_call_target="tpu_custom_call" | custom-call | tf_op jit(solution)/shard_map/total/pallas_call | solution.py:180
  187.7 0.5 slice.15
  188.2 0.5 slice_bitcast_fusion
  188.8 0.7 copy.43
  189.5 0.8 copy.42
  191.0 0.7 copy.47
  191.7 0.7 copy.48
  (33 shorter events, 0.6 us)
Async XLA Ops:
  7.2 106.7 %all-gather.2.cloned.1.call-start = ((), (), s32[]{:S(2)}) async-start(), calls=%async_computation | async-start | bytes 1081344 | tf_op jit(solution)/shard_map/all_gather | solution.py:393
  9.6 1.6 copy-start
  11.2 0.9 copy-start.2
  12.1 0.9 copy-start.4
  13.0 0.9 copy-start.6
  13.9 0.7 copy-start.8
  14.5 0.7 copy-start.10
  21.8 13.0 %collective-permute-start.1 = (bf16[16,64,128]{2,1,0:T(8,128)(2,1)S(1)}, bf16[16,64,128]{2,1,0:T(8,128)(2,1)S(1)}, u32[]{:S(2)}, u32[]{:S(2)}) collective-permute-start(bf16[16,64,128]{2,1,0:T(8,128)(2,1)S(1)} %get-tuple-element.76), channel_id=1, source_target_pairs={{0,4},{1,12},{2,20},{3,28},{4,0},{5,8},{6,16},{7,24},{8,5},{9,13},... | collective-permute-start | bytes 786440 | tf_op jit(solution)/shard_map/ppermute | solution.py:280
  22.3 12.5 %collective-permute-start = (bf16[16,64,128]{2,1,0:T(8,128)(2,1)S(1)}, bf16[16,64,128]{2,1,0:T(8,128)(2,1)}, u32[]{:S(2)}, u32[]{:S(2)}) collective-permute-start(bf16[16,64,128]{2,1,0:T(8,128)(2,1)S(1)} %get-tuple-element.77), channel_id=1, source_target_pairs={{0,0},{1,8},{2,16},{3,24},{4,4},{5,12},{6,20},{7,28},{8,1},{9,9},{... | collective-permute-start | bytes 786440 | tf_op jit(solution)/shard_map/ppermute | solution.py:280
  30.3 4.5 %collective-permute-start.3 = (bf16[16,64,128]{2,1,0:T(8,128)(2,1)S(1)}, bf16[16,64,128]{2,1,0:T(8,128)(2,1)}, u32[]{:S(2)}, u32[]{:S(2)}) collective-permute-start(bf16[16,64,128]{2,1,0:T(8,128)(2,1)S(1)} %get-tuple-element.72), channel_id=1, source_target_pairs={{0,4},{1,12},{2,20},{3,28},{4,0},{5,8},{6,16},{7,24},{8,5},{9,13},... | collective-permute-start | bytes 786440 | tf_op jit(solution)/shard_map/ppermute | solution.py:280
  30.4 4.4 %collective-permute-start.2 = (bf16[16,64,128]{2,1,0:T(8,128)(2,1)S(1)}, bf16[16,64,128]{2,1,0:T(8,128)(2,1)}, u32[]{:S(2)}, u32[]{:S(2)}) collective-permute-start(bf16[16,64,128]{2,1,0:T(8,128)(2,1)S(1)} %get-tuple-element.73), channel_id=1, source_target_pairs={{0,0},{1,8},{2,16},{3,24},{4,4},{5,12},{6,20},{7,28},{8,1},{9,9},{... | collective-permute-start | bytes 786440 | tf_op jit(solution)/shard_map/ppermute | solution.py:280
  34.8 81.2 %copy-start.3 = (bf16[128,512]{1,0:T(8,128)(2,1)S(1)}, bf16[128,512]{1,0:T(8,128)(2,1)}, u32[]{:S(2)}) copy-start(bf16[128,512]{1,0:T(8,128)(2,1)} %refs_7_.3) | copy-start | bytes 393220
  34.8 81.2 %copy-start.5 = (bf16[128,512]{1,0:T(8,128)(2,1)S(1)}, bf16[128,512]{1,0:T(8,128)(2,1)}, u32[]{:S(2)}) copy-start(bf16[128,512]{1,0:T(8,128)(2,1)} %refs_8_.3) | copy-start | bytes 393220
  34.8 81.2 %copy-start.7 = (bf16[512,128]{1,0:T(8,128)(2,1)S(1)}, bf16[512,128]{1,0:T(8,128)(2,1)}, u32[]{:S(2)}) copy-start(bf16[512,128]{1,0:T(8,128)(2,1)} %refs_9_.3) | copy-start | bytes 393220
  34.8 81.2 %copy-start.9 = (f32[128]{0:T(128)S(1)}, f32[128]{0:T(128)}, u32[]{:S(2)}) copy-start(f32[128]{0:T(128)} %param.10) | copy-start | bytes 1540
  34.9 81.2 %copy-start.11 = (f32[128]{0:T(128)S(1)}, f32[128]{0:T(128)}, u32[]{:S(2)}) copy-start(f32[128]{0:T(128)} %param.11) | copy-start | bytes 1540
  116.0 1.6 copy-start.1
Sparse Core Ops, SparseCore 0:
  11.6 102.3 all-gather.1

commit v3 on v2

--- a/solution.py
+++ b/solution.py
@@ -265,13 +265,12 @@
 def mirror(packed_part):
     across, down = lax.axis_size("row"), lax.axis_size("col")
     fold = across // down
-    deep, cols_tile, bins = packed_part.shape
-    edge = cols_tile // fold
+    edge = packed_part.shape[1] // fold
     place = lax.axis_index("row")
     came = []
     for turn in range(fold):
         sub = lax.rem(place + turn, fold)
-        packed = lax.dynamic_slice(packed_part, (0, sub * edge, 0), (deep, edge, bins))
+        packed = lax.dynamic_slice_in_dim(packed_part, sub * edge, edge, 1)
         pairs = [
             (r * down + c, (c * fold + (r + turn) % fold) * down + r // fold)
             for r in range(across)
@@ -390,10 +389,8 @@
     deep = rows_tile // pieces
 
     code = jnp.where(pair_mask > 0, targets, -1)
-    codes = lax.all_gather(code, ("row", "col"), axis=0, tiled=True)
-    top, side = lax.axis_index("row") * rows_tile, lax.axis_index("col") * cols_tile
-    code_tile = lax.dynamic_slice(codes, (top, side), (rows_tile, cols_tile))
-    code_turn = lax.dynamic_slice(codes, (side, top), (cols_tile, rows_tile)).T
+    code_tile = lax.all_to_all(code, "col", split_axis=1, concat_axis=0, tiled=True)
+    turned = jnp.swapaxes(ordered(mirror(code_tile)), 1, 2)
 
     outs, arrivals = [], []
     for piece in range(pieces):
@@ -416,7 +413,9 @@
         jnp.zeros((8, width), jnp.float32),
     ]
     weights = [ln_gain[None], ln_bias[None], gate_weight, up_weight, out_weight, head_weight]
-    codes_here, codes_turn = by_columns(code_tile), by_columns(code_turn)
+    codes_here = by_columns(code_tile)
+    codes_turn = jnp.swapaxes(turned.reshape(fold, rows_tile, pieces, deep), 1, 2)
+    codes_turn = codes_turn.reshape(fold * pieces, rows_tile, deep)
     for piece in range(pieces):
         totals = backward(
             piece,

time: 201 us -> 181 us (0.900)
  waiting for transfers between devices: 77.4 us -> 0.02 us
  Pallas kernels: 83.1 us -> 148 us
  between operations: 16.1 us -> 2.74 us
  starting transfers between devices: 3.38 us -> 10.4 us
  local copies, waits for them, and re-layouts: 14.1 us -> 11.5 us
    all_gather x1 -> x0, waiting for transfers between devices: 77.3 us -> none  [shards(): codes = lax.all_gather(code, ('row', 'col'), axis=0, tiled=True)]
    pallas_call x1, Pallas kernels: 27.9 us -> 92.9 us  [total(): pl.pallas_call(functools.partial(total_kernel, bits, parts, shapes), out_...]
    all_to_all x0 -> x1, starting transfers between devices: none -> 6.32 us  [shards(): lax.all_to_all(code, 'col', split_axis=1, concat_axis=0, tiled=True)]
    unnamed x30 -> x29, local copies, waits for them, and re-layouts: 11.1 us -> 9.42 us
    ppermute x4 -> x6, starting transfers between devices: 3.34 us -> 4.13 us  [mirror(): came.append(lax.ppermute(packed, ('row', 'col'), pairs))]
  transfers between devices with their start and end apart: 5 -> 7, of which waited for: 1 -> 0; matrix products, arithmetic and copies ran while one was open for 3% -> 3% of each run, Pallas kernels for 7% -> 7%
where the time goes in v3:
time: 181 us; the launch traced here: 180 us
  Pallas kernels  148 us (82%)
  local copies, waits for them, and re-layouts  11.5 us (6%)
  starting transfers between devices  10.4 us (6%)
  other arithmetic  7.14 us (4%)
  between operations  2.74 us (2%)
    pallas_call x1, Pallas kernels, total(): pl.pallas_call(functools.partial(total_kernel, bits, parts, shapes), out_...  92.9 us
    pallas_call x2, Pallas kernels, backward(): pl.pallas_call(functools.partial(backward_kernel, tokens), grid=(fold, ro...  42.4 us
    pallas_call x2, Pallas kernels, forward(): pl.pallas_call(forward_kernel, grid=(deep // 2 // group,), out_shape=[jax...  13.1 us
    unnamed x29, local copies, waits for them, and re-layouts  9.42 us
    all_to_all x1, starting transfers between devices, shards(): lax.all_to_all(code, 'col', split_axis=1, concat_axis=0, tiled=True)  6.32 us
    ppermute x6, starting transfers between devices, mirror(): came.append(lax.ppermute(packed, ('row', 'col'), pairs))  4.13 us
  transfers between devices with their start and end apart: 7, of which 0 were waited for; matrix products, arithmetic and copies ran while one was open for 3% of the time, Pallas kernels for 7%

profile of v3, /device:TPU:0, one launch (start us, length us, event | category | flops | bytes accessed | tf_op | source)
XLA Modules:
  0.0 180.3 jit_solution(15338909160022576960)
XLA Ops:
  0.6 1.4 copy_bitcast_fusion.1
  2.0 6.3 %all-to-all-start = ((s32[16,4,128]{2,0,1:T(8,128)}), s32[16,4,128]{2,0,1:T(8,128)S(1)}, u32[]{:S(2)}, u32[]{:S(2)}) async-start(s32[16,4,128]{2,0,1:T(8,128)} %copy_bitcast_fusion.1), calls=%async_computation | async-start | bytes 65536 | tf_op jit(solution)/shard_map/all_to_all | solution.py:392
  8.3 0.8 copy.42.refs_10_
  9.2 0.1 fusion.6.both_ref
  9.3 1.6 copy-done
  10.9 0.9 copy-done.2
  11.8 0.9 copy-done.4
  12.7 0.9 copy-done.6
  13.6 0.7 copy-done.8
  14.2 0.7 copy-done.10
  14.9 6.6 %forward.3 = (bf16[2,16,128,128]{3,2,1,0:T(8,128)(2,1)S(1)}, bf16[16,128,128]{2,1,0:T(8,128)(2,1)S(1)}) custom-call(bf16[4,16,128,128]{3,2,1,0:T(8,128)(2,1)S(1)} %bitcast.43, f32[1,128]{1,0:T(1,128)S(1)} %bitcast.47, f32[1,128]{1,0:T(1,128)S(1)} %bitcast.51, bf16[128,512]{1,0:T(8,128)(2,1)S(1)} %copy-done.2, bf16[128,512]{1,0:T(8,128)(2,1)S(1)} %copy-done.4, ...), custom_call_target="tpu_custom_call" | custom-call | flops 1610612736 | bytes 3145728 | tf_op jit(solution)/shard_map/forward/pallas_call | solution.py:236
  21.6 1.4 collective-permute-start
  23.0 6.6 %forward.2 = (bf16[2,16,128,128]{3,2,1,0:T(8,128)(2,1)S(1)}, bf16[16,128,128]{2,1,0:T(8,128)(2,1)S(1)}) custom-call(bf16[4,16,128,128]{3,2,1,0:T(8,128)(2,1)S(1)} %bitcast.44, f32[1,128]{1,0:T(1,128)S(1)} %bitcast.48, f32[1,128]{1,0:T(1,128)S(1)} %bitcast.52, bf16[128,512]{1,0:T(8,128)(2,1)S(1)} %copy-done.2, bf16[128,512]{1,0:T(8,128)(2,1)S(1)} %copy-done.4, ...), custom_call_target="tpu_custom_call" | custom-call | flops 1610612736 | bytes 3145728 | tf_op jit(solution)/shard_map/forward/pallas_call | solution.py:236
  29.6 0.6 collective-permute-start.5
  30.1 1.5 pad_maximum_fusion.1.refs_1_
  31.7 0.7 constant_dynamic-slice_fusion.2
  32.4 1.2 collective-permute-start.2
  33.6 1.5 pad_maximum_fusion
  35.1 0.1 reshape.53
  35.3 0.9 collective-permute-start.4
  36.2 0.8 fusion.8
  37.1 0.1 copy.46
  37.3 1.6 fusion.1
  39.1 21.2 %backward.2 = (f32[128,512]{1,0:T(8,128)S(1)}, f32[128,512]{1,0:T(8,128)S(1)}, f32[128,512]{1,0:T(8,128)S(1)}, f32[128,128]{1,0:T(8,128)S(1)}, f32[8,128]{1,0:T(8,128)S(1)}) custom-call(bf16[64,4,32,128]{3,2,1,0:T(8,128)(2,1)S(1)} %bitcast.45, bf16[64,4,32,128]{3,2,1,0:T(8,128)(2,1)} %pad_maximum_fusion.1.refs_1_, ...), custom_call_target="tpu_custom_call" | custom-call | flops 4294967296 | bytes 4194304 | tf_op jit(solution)/shard_map/backward/pallas_call | solution.py:363
  60.2 21.2 %backward.3 = (f32[128,512]{1,0:T(8,128)S(1)}, f32[128,512]{1,0:T(8,128)S(1)}, f32[128,512]{1,0:T(8,128)S(1)}, f32[128,128]{1,0:T(8,128)S(1)}, f32[8,128]{1,0:T(8,128)S(1)}) custom-call(bf16[64,4,32,128]{3,2,1,0:T(8,128)(2,1)S(1)} %bitcast.46, bf16[64,4,32,128]{3,2,1,0:T(8,128)(2,1)} %pad_maximum_fusion.1.refs_1_, ...), custom_call_target="tpu_custom_call" | custom-call | flops 4294967296 | bytes 4194304 | tf_op jit(solution)/shard_map/backward/pallas_call | solution.py:363
  81.5 92.9 %total.1 = (f32[128,512]{1,0:T(8,128)S(1)}, f32[128,512]{1,0:T(8,128)S(1)}, f32[128,512]{1,0:T(8,128)S(1)}, f32[128,128]{1,0:T(8,128)S(1)}, f32[8,128]{1,0:T(8,128)S(1)}) custom-call(f32[128,512]{1,0:T(8,128)S(1)} %get-tuple-element.36.refs_0_, f32[128,512]{1,0:T(8,128)S(1)} %get-tuple-element.37.refs_1_, f32[128,512]{1,0:T(8,128)S(1)} %get-tuple-element.38.refs_2_, ...), custom_call_target="tpu_custom_call" | custom-call | tf_op jit(solution)/shard_map/total/pallas_call | solution.py:180
  174.4 0.5 slice.23
  174.9 0.5 slice_bitcast_fusion
  175.5 0.7 copy.50
  176.2 0.8 copy.49
  177.7 0.7 copy.57
  178.4 0.7 copy.58
  (39 shorter events, 0.6 us)
Async XLA Ops:
  2.0 29.6 %all-to-all-start = ((s32[16,4,128]{2,0,1:T(8,128)}), s32[16,4,128]{2,0,1:T(8,128)S(1)}, u32[]{:S(2)}, u32[]{:S(2)}) async-start(s32[16,4,128]{2,0,1:T(8,128)} %copy_bitcast_fusion.1), calls=%async_computation | async-start | bytes 65536 | tf_op jit(solution)/shard_map/all_to_all | solution.py:392
  9.3 1.6 copy-start
  10.9 0.9 copy-start.2
  11.8 0.9 copy-start.4
  12.7 0.9 copy-start.6
  13.6 0.7 copy-start.8
  14.2 0.7 copy-start.10
  21.5 15.7 %collective-permute-start.1 = (bf16[16,64,128]{2,1,0:T(8,128)(2,1)S(1)}, bf16[16,64,128]{2,1,0:T(8,128)(2,1)S(1)}, u32[]{:S(2)}, u32[]{:S(2)}) collective-permute-start(bf16[16,64,128]{2,1,0:T(8,128)(2,1)S(1)} %get-tuple-element.84), channel_id=1, source_target_pairs={{0,4},{1,12},{2,20},{3,28},{4,0},{5,8},{6,16},{7,24},{8,5},{9,13},... | collective-permute-start | bytes 786440 | tf_op jit(solution)/shard_map/ppermute | solution.py:279
  21.6 15.6 %collective-permute-start = (bf16[16,64,128]{2,1,0:T(8,128)(2,1)S(1)}, bf16[16,64,128]{2,1,0:T(8,128)(2,1)}, u32[]{:S(2)}, u32[]{:S(2)}) collective-permute-start(bf16[16,64,128]{2,1,0:T(8,128)(2,1)S(1)} %get-tuple-element.85), channel_id=1, source_target_pairs={{0,0},{1,8},{2,16},{3,24},{4,4},{5,12},{6,20},{7,28},{8,1},{9,9},{... | collective-permute-start | bytes 786440 | tf_op jit(solution)/shard_map/ppermute | solution.py:279
  29.6 7.6 %collective-permute-start.5 = (bf16[16,64,128]{2,1,0:T(8,128)(2,1)S(1)}, bf16[16,64,128]{2,1,0:T(8,128)(2,1)}, u32[]{:S(2)}, u32[]{:S(2)}) collective-permute-start(bf16[16,64,128]{2,1,0:T(8,128)(2,1)S(1)} %get-tuple-element.80), channel_id=1, source_target_pairs={{0,4},{1,12},{2,20},{3,28},{4,0},{5,8},{6,16},{7,24},{8,5},{9,13},... | collective-permute-start | bytes 786440 | tf_op jit(solution)/shard_map/ppermute | solution.py:279
  32.4 2.9 %collective-permute-start.3 = (s32[64,64]{1,0:T(8,128)}, s32[64,64]{1,0:T(8,128)S(1)}, u32[]{:S(2)}, u32[]{:S(2)}) collective-permute-start(s32[64,64]{1,0:T(8,128)} %get-tuple-element.90), channel_id=1, source_target_pairs={{0,4},{1,12},{2,20},{3,28},{4,0},{5,8},{6,16},{7,24},{8,5},{9,13},... | collective-permute-start | bytes 49160 | tf_op jit(solution)/shard_map/ppermute | solution.py:279
  32.4 3.8 %collective-permute-start.2 = (s32[64,64]{1,0:T(8,128)S(1)}, s32[64,64]{1,0:T(8,128)}, u32[]{:S(2)}, u32[]{:S(2)}) collective-permute-start(s32[64,64]{1,0:T(8,128)S(1)} %get-tuple-element.91), channel_id=1, source_target_pairs={{0,0},{1,8},{2,16},{3,24},{4,4},{5,12},{6,20},{7,28},{8,1},{9,9},{... | collective-permute-start | bytes 49160 | tf_op jit(solution)/shard_map/ppermute | solution.py:279
  35.3 1.9 %collective-permute-start.4 = (bf16[16,64,128]{2,1,0:T(8,128)(2,1)S(1)}, bf16[16,64,128]{2,1,0:T(8,128)(2,1)S(1)}, u32[]{:S(2)}, u32[]{:S(2)}) collective-permute-start(bf16[16,64,128]{2,1,0:T(8,128)(2,1)S(1)} %get-tuple-element.81), channel_id=1, source_target_pairs={{0,0},{1,8},{2,16},{3,24},{4,4},{5,12},{6,20},{7,28},{8,1},{9,9},{... | collective-permute-start | bytes 786440 | tf_op jit(solution)/shard_map/ppermute | solution.py:279
  37.2 1.8 %copy-start.1 = (bf16[64,128,128]{2,1,0:T(8,128)(2,1)S(1)}, bf16[64,128,128]{2,1,0:T(8,128)(2,1)}, u32[]{:S(2)}) copy-start(bf16[64,128,128]{2,1,0:T(8,128)(2,1)} %param.9) | copy-start | bytes 6291460
  37.2 1.8 %copy-start.3 = (bf16[128,512]{1,0:T(8,128)(2,1)S(1)}, bf16[128,512]{1,0:T(8,128)(2,1)}, u32[]{:S(2)}) copy-start(bf16[128,512]{1,0:T(8,128)(2,1)} %refs_7_.3) | copy-start | bytes 393220
  37.2 1.8 %copy-start.5 = (bf16[128,512]{1,0:T(8,128)(2,1)S(1)}, bf16[128,512]{1,0:T(8,128)(2,1)}, u32[]{:S(2)}) copy-start(bf16[128,512]{1,0:T(8,128)(2,1)} %refs_8_.3) | copy-start | bytes 393220
  37.2 1.8 %copy-start.7 = (bf16[512,128]{1,0:T(8,128)(2,1)S(1)}, bf16[512,128]{1,0:T(8,128)(2,1)}, u32[]{:S(2)}) copy-start(bf16[512,128]{1,0:T(8,128)(2,1)} %refs_9_.3) | copy-start | bytes 393220
  37.3 1.8 %copy-start.9 = (f32[128]{0:T(128)S(1)}, f32[128]{0:T(128)}, u32[]{:S(2)}) copy-start(f32[128]{0:T(128)} %param.10) | copy-start | bytes 1540
  37.3 1.8 %copy-start.11 = (f32[128]{0:T(128)S(1)}, f32[128]{0:T(128)}, u32[]{:S(2)}) copy-start(f32[128]{0:T(128)} %param.11) | copy-start | bytes 1540
